TPU v7x, 32 devices: a whole 2x2x4 slice. The times are simulated.
32 devices in a mesh: seq: 8 (over z, x), head: 4 (over y, core).
Axes of the slice: x: 2, y: 2, z: 4, core: 2. Of those that a mesh axis runs over, the one named last changes fastest.
Arguments:
- queries: bfloat16 [2048, 16, 128], P(('seq', 'head')), may hold values from -6 to 6
- key_vectors: bfloat16 [2048, 16, 128], P(('seq', 'head')), may hold values from -6 to 6
- value_vectors: bfloat16 [2048, 32, 128], P(('seq', 'head')), may hold values from -6 to 6
- output_gate: bfloat16 [2048, 32, 128], P(('seq', 'head')), may hold values from -6 to 6
- write_strength: bfloat16 [2048, 32], P(('seq', 'head'))
- norm_gain: bfloat16 [128], replicated, may hold values from 0.099609375 to 1.8984375
- output_weight: bfloat16 [4096, 2048], P('head'), may hold values from -0.09375 to 0.09375
Outputs:
- projected: bfloat16 [2048, 2048], P(('seq', 'head'))
All inputs are finite; a program needn't handle non-finite values.
Results may differ from a plain program's by a relative error of at most 0.017.
Values may be sent and summed in bfloat16 or wider, within the bound.
No kernel may reach another device: no remote copies, remote signals or barrier semaphores. Data moves between devices by JAX's collectives and lax.ppermute only.
A program may use at most 128 MiB of HBM per device.

v0:
```python
import functools

import jax
import jax.numpy as jnp
from jax import lax
from jax.experimental import pallas as pl
from jax.experimental.pallas import tpu as pltpu
from jax.sharding import Mesh, PartitionSpec as P

SPAN = 128
EPSILON = 1e-06
F32 = jnp.float32
BF16 = jnp.bfloat16
ROW_TILE = 16
VMEM = pl.BlockSpec(memory_space=pltpu.VMEM)
SMEM = pl.BlockSpec(memory_space=pltpu.SMEM)
ANY = pl.BlockSpec(memory_space=pl.ANY)


def dot(left, right):
    return jnp.dot(left, right, preferred_element_type=F32)


def dot_nt(left, right):
    return lax.dot_general(left, right, (((1,), (1,)), ((), ())), preferred_element_type=F32)


def params(megabytes=48):
    return pltpu.CompilerParams(vmem_limit_bytes=megabytes * 2**20)


def turned(ref):
    return jnp.transpose(ref[...], (1, 0, 2))


def pack_write_kernel(sub, k_hbm, v_hbm, b_hbm, out_ref, k_ref, v_ref, b_ref, done):
    tokens, key_heads, width = k_ref.shape
    value_heads = v_ref.shape[1]
    ratio = value_heads // key_heads
    n_head = key_heads // sub
    copies = [
        pltpu.make_async_copy(source, target, done.at[place])
        for place, (source, target) in enumerate(((b_hbm, b_ref), (k_hbm, k_ref), (v_hbm, v_ref)))
    ]
    for copy in copies:
        copy.start()
    copies[0].wait()
    strength = jnp.concatenate([b_ref[...].astype(F32)] * (width // tokens), axis=1)
    strength = jnp.concatenate([strength, jnp.zeros((ROW_TILE, width), F32)], axis=0)
    copies[1].wait()
    k_t = turned(k_ref)
    heads = [(peer % n_head) * sub + peer // n_head for peer in range(key_heads)]
    for peer, head in enumerate(heads):
        out_ref[peer, 0:tokens] = k_t[head]
        out_ref[peer, (1 + ratio) * tokens :] = strength[
            head * ratio : head * ratio + ROW_TILE
        ].astype(BF16)
    copies[2].wait()
    v_t = turned(v_ref)
    for peer, head in enumerate(heads):
        for r in range(ratio):
            out_ref[peer, (1 + r) * tokens : (2 + r) * tokens] = v_t[head * ratio + r]


def pack_read_kernel(sub, q_hbm, g_hbm, out_ref, q_ref, g_ref, done):
    tokens, key_heads, width = q_ref.shape
    ratio = g_ref.shape[1] // key_heads
    n_head = key_heads // sub
    copies = [
        pltpu.make_async_copy(source, target, done.at[place])
        for place, (source, target) in enumerate(((q_hbm, q_ref), (g_hbm, g_ref)))
    ]
    for copy in copies:
        copy.start()
    heads = [(peer % n_head) * sub + peer // n_head for peer in range(key_heads)]
    copies[0].wait()
    q_t = turned(q_ref)
    for peer, head in enumerate(heads):
        out_ref[peer, 0:tokens] = q_t[head]
    copies[1].wait()
    g_t = turned(g_ref)
    for peer, head in enumerate(heads):
        for r in range(ratio):
            out_ref[peer, (1 + r) * tokens : (2 + r) * tokens] = g_t[head * ratio + r]


def block_rows(got_ref, block, per, tokens, part):
    rows = got_ref[pl.ds(block * per, per), part * tokens : (part + 1) * tokens]
    return rows.reshape(per * tokens, rows.shape[-1])


def block_inverse(below):
    size = below[0].shape[0]
    rows = lax.broadcasted_iota(jnp.int32, (size, size), 0)
    cols = lax.broadcasted_iota(jnp.int32, (size, size), 1)
    zero = jnp.zeros((size, size), F32)
    step = 1
    solved = None
    while step < size:
        joins = (rows // (2 * step) == cols // (2 * step)) & (rows // step > cols // step)
        parts = [jnp.where(joins, matrix, zero) for matrix in below]
        if step == 1:
            solved = [
                jnp.where(rows == cols, jnp.ones_like(zero), -part).astype(BF16) for part in parts
            ]
        else:
            inner = [dot(part.astype(BF16), now).astype(BF16) for part, now in zip(parts, solved)]
            solved = [now - dot(now, mid).astype(BF16) for now, mid in zip(solved, inner)]
        step *= 2
    return solved


def factor_kernel(tokens, ratio, group, got_ref, state_ref, w_ref, u_ref, trans_ref, prefix_ref, add_ref):
    width = got_ref.shape[-1]
    per = SPAN // tokens
    blocks = got_ref.shape[0] // per
    rows = lax.broadcasted_iota(jnp.int32, (SPAN, SPAN), 0)
    cols = lax.broadcasted_iota(jnp.int32, (SPAN, SPAN), 1)
    lane = lax.broadcasted_iota(jnp.int32, (1, SPAN), 1)
    first = (1 + ratio) * tokens

    def factors(outer):
        below, held = [], []
        for inner in range(group):
            block = outer * group + inner
            key = block_rows(got_ref, block, per, tokens, 0)
            gram = dot_nt(key, key)
            squares = jnp.where(rows == cols, gram, 0.0)
            key_row = lax.rsqrt(jnp.sum(squares, 0, keepdims=True) + EPSILON)
            key_col = lax.rsqrt(jnp.sum(squares, 1, keepdims=True) + EPSILON)
            lower = jnp.where(rows > cols, gram, 0.0) * key_row
            for r in range(ratio):
                strength = jnp.zeros((1, SPAN), F32)
                for place in range(per):
                    piece = got_ref[block * per + place, first : first + ROW_TILE].astype(F32)[r : r + 1]
                    strength = jnp.where(lane // tokens == place, piece, strength)
                scaled_col = jnp.sum(jnp.where(rows == cols, strength * key_row, 0.0), 1, keepdims=True)
                below.append(lower * scaled_col)
                held.append((block, r, key, key_col, key_row, strength))
        solved = block_inverse(below)
        for now, (block, r, key, key_col, key_row, strength) in zip(solved, held):
            value = block_rows(got_ref, block, per, tokens, 1 + r)
            weighted = now.astype(F32) * key_col * strength
            u_now = dot(weighted.astype(BF16), value)
            w_now = dot((weighted * key_row).astype(BF16), key).astype(BF16)
            both = dot(key.T, jnp.concatenate([w_now, u_now.astype(BF16)], axis=1))
            w_ref[block, r] = w_now
            u_ref[block, r] = u_now
            trans_ref[block, r] = both[:, :width].astype(BF16)
            add_ref[block, r] = both[:, width:]

    for outer in range(blocks // group):
        factors(outer)

    states = [jnp.zeros((width, width), F32) for r in range(ratio)]
    for block in range(blocks):
        for r in range(ratio):
            held = states[r].astype(BF16)
            prefix_ref[block, r] = held
            if block == 0:
                states[r] = add_ref[block, r]
            else:
                states[r] = states[r] + add_ref[block, r] - dot(trans_ref[block, r], held)
    for r in range(ratio):
        state_ref[r] = states[r].astype(state_ref.dtype)


def spread_kernel(
    tokens, ratio, got_ref, read_ref, w_ref, u_ref, trans_ref, prefix_ref, local_ref, reach_ref, total_ref
):
    width = got_ref.shape[-1]
    per = SPAN // tokens
    blocks = got_ref.shape[0] // per
    rows = lax.broadcasted_iota(jnp.int32, (SPAN, SPAN), 0)
    cols = lax.broadcasted_iota(jnp.int32, (SPAN, SPAN), 1)
    wide_rows = lax.broadcasted_iota(jnp.int32, (width, width), 0)
    wide_cols = lax.broadcasted_iota(jnp.int32, (width, width), 1)
    identity = jnp.where(wide_rows == wide_cols, 1.0, 0.0).astype(F32)
    carried = [identity for r in range(ratio)]
    for block in range(blocks):
        query = block_rows(read_ref, block, per, tokens, 0)
        key = block_rows(got_ref, block, per, tokens, 0)
        scores = jnp.where(rows >= cols, dot_nt(query, key), 0.0).astype(BF16)
        query_f = query.astype(F32)
        squares = jnp.sum(query_f * query_f, 1, keepdims=True)
        unit = lax.rsqrt(squares + EPSILON) * width ** (-0.5)
        left = jnp.concatenate([query, scores], axis=1)
        for r in range(ratio):
            held = carried[r].astype(BF16)
            if block == 0:
                carried[r] = identity - trans_ref[block, r].astype(F32)
            else:
                carried[r] = carried[r] - dot(trans_ref[block, r], held)
            starts = jnp.concatenate([prefix_ref[block, r], held], axis=1)
            passed = dot(w_ref[block, r], starts)
            corrected = jnp.concatenate([u_ref[block, r] - passed[:, :width], -passed[:, width:]], axis=1)
            right = jnp.concatenate([starts, corrected.astype(BF16)], axis=0)
            out = dot(left, right) * unit
            local_ref[r, block] = out[:, :width]
            reach_ref[r, block] = out[:, width:].astype(BF16)
    for r in range(ratio):
        total_ref[r] = carried[r]


def join_kernel(tokens, place_ref, state_ref, local_ref, reach_ref, read_ref, gain_ref, *out_refs):
    ratio, blocks, span, width = local_ref.shape
    per = span // tokens
    pieces = blocks // len(out_refs)
    gain = gain_ref[...].astype(F32)
    mine = place_ref[0]
    for distance, out_ref in enumerate(out_refs):
        target = mine ^ distance
        for piece in range(pieces):
            block = target * pieces + piece
            for r in range(ratio):
                core = local_ref[r, block] + dot(reach_ref[r, block], state_ref[r].astype(BF16))
                mean_square = jnp.mean(core * core, 1, keepdims=True)
                gate = block_rows(read_ref, block, per, tokens, 1 + r).astype(F32)
                gated = core * lax.rsqrt(mean_square + EPSILON) * gain * (gate / (1.0 + jnp.exp(-gate)))
                out_ref[piece, r] = gated.astype(BF16)


def project_kernel(tokens, parts, place_ref, *refs):
    gated_refs, weight_ref, send_ref, keep_ref, rows_ref = refs[:parts], refs[parts], *refs[parts + 1 :]
    pieces, ratio, span, width = gated_refs[0].shape
    per = span // tokens
    half = pieces * per // 2

    @pl.when(pl.program_id(0) == 0)
    def _():
        for distance, gated_ref in enumerate(gated_refs):
            source = place_ref[0] ^ distance
            for r in range(ratio):
                lanes = pl.ds(pl.multiple_of((source * ratio + r) * width, width), width)
                for kept in range(2):
                    for place in range(half):
                        share = 2 * place + ((place_ref[1] + 1 + kept) & 1)
                        block = gated_ref[share // per, r, pl.ds(pl.multiple_of(share % per * tokens, tokens), tokens)]
                        first = (kept * half + place) * tokens
                        rows_ref[first : first + tokens, lanes] = block

    out = dot(rows_ref[...], weight_ref[...]).reshape(2, half, tokens, weight_ref.shape[1])
    send_ref[...] = out[0].astype(BF16)
    keep_ref[...] = out[1]


def halve_kernel(stage, place_ref, keep_ref, got_ref, send_ref, left_ref):
    bit = (place_ref[1] >> stage) & 1
    for place in range(keep_ref.shape[0] // 2):
        there, here = 2 * place + 1 - bit, 2 * place + bit
        send_ref[place] = (keep_ref[there] + got_ref[there].astype(F32)).astype(BF16)
        left_ref[place] = keep_ref[here] + got_ref[here].astype(F32)


def per_device(
    outer, sub, n_head, queries, key_vectors, value_vectors, output_gate, write_strength, norm_gain, output_weight
):
    tokens, key_heads, width = queries.shape
    value_heads = value_vectors.shape[1]
    ratio = value_heads // key_heads
    sources = sub * n_head
    shard = tokens * sources
    blocks = shard // SPAN
    shard_tokens = tokens * n_head
    shape = jax.ShapeDtypeStruct
    place = jnp.stack([lax.axis_index("sub"), lax.axis_index("head")]).astype(jnp.int32)

    with jax.named_scope("pack_write"):
        write = pl.pallas_call(
            functools.partial(pack_write_kernel, sub),
            out_shape=shape((sources, (1 + ratio) * tokens + ROW_TILE, width), BF16),
            in_specs=[ANY] * 3,
            out_specs=VMEM,
            scratch_shapes=[
                pltpu.VMEM(key_vectors.shape, BF16),
                pltpu.VMEM(value_vectors.shape, BF16),
                pltpu.VMEM((value_heads, tokens), BF16),
                pltpu.SemaphoreType.DMA((3,)),
            ],
            compiler_params=params(60),
        )(key_vectors, value_vectors, write_strength.T)
    got = lax.all_to_all(write, ("sub", "head"), split_axis=0, concat_axis=0, tiled=True)
    with jax.named_scope("pack_read"):
        read = pl.pallas_call(
            functools.partial(pack_read_kernel, sub),
            out_shape=shape((sources, (1 + ratio) * tokens, width), BF16),
            in_specs=[ANY] * 2,
            out_specs=VMEM,
            scratch_shapes=[
                pltpu.VMEM(queries.shape, BF16),
                pltpu.VMEM(output_gate.shape, BF16),
                pltpu.SemaphoreType.DMA((2,)),
            ],
            compiler_params=params(60),
        )(queries, output_gate)
    got_read = lax.all_to_all(read, ("sub", "head"), split_axis=0, concat_axis=0, tiled=True)

    state_type = BF16 if outer == 2 else F32
    square = (blocks, ratio, width, width)
    with jax.named_scope("factors"):
        state, w, u, trans, prefix = pl.pallas_call(
            functools.partial(factor_kernel, tokens, ratio, blocks),
            out_shape=[
                shape((ratio, width, width), state_type),
                shape((blocks, ratio, SPAN, width), BF16),
                shape((blocks, ratio, SPAN, width), F32),
                shape(square, BF16),
                shape(square, BF16),
            ],
            in_specs=[VMEM],
            out_specs=[VMEM] * 5,
            scratch_shapes=[pltpu.VMEM(square, F32)],
            compiler_params=params(),
            cost_estimate=pl.CostEstimate(flops=5 * 10**9, bytes_accessed=4 * 10**6, transcendentals=0),
        )(got)

    onward = [(here, here + 1) for here in range(outer - 1)]
    incoming = lax.ppermute(state, "outer", onward)
    with jax.named_scope("spread"):
        local, reach, total = pl.pallas_call(
            functools.partial(spread_kernel, tokens, ratio),
            out_shape=[
                shape((ratio, blocks, SPAN, width), F32),
                shape((ratio, blocks, SPAN, width), BF16),
                shape((ratio, width, width), F32),
            ],
            in_specs=[VMEM] * 6,
            out_specs=[VMEM] * 3,
            compiler_params=params(),
            cost_estimate=pl.CostEstimate(flops=10**9, bytes_accessed=8 * 10**6, transcendentals=0),
        )(got, got_read, w, u, trans, prefix)
    for hop in range(outer - 2):
        passed = jnp.einsum("hde,hef->hdf", total, incoming, precision=lax.Precision.HIGHEST)
        incoming = lax.ppermute(state + passed, "outer", onward)

    pieces = shard_tokens // SPAN
    with jax.named_scope("join"):
        gated = pl.pallas_call(
            functools.partial(join_kernel, tokens),
            out_shape=[shape((pieces, ratio, SPAN, width), BF16)] * sub,
            in_specs=[SMEM] + [VMEM] * 5,
            out_specs=[VMEM] * sub,
            compiler_params=params(),
        )(place, incoming, local, reach, got_read, norm_gain.reshape(1, width))
    gated = list(gated)
    for distance in reversed(range(1, sub)):
        pairs = [(here, here ^ distance) for here in range(sub)]
        gated[distance] = lax.ppermute(gated[distance], "sub", pairs)

    columns = output_weight.shape[1]
    tile = 512
    chunks = 2
    steps = columns // chunks // tile
    depth = sub * ratio * width
    half = n_head // 2
    summed = []
    for chunk in range(chunks):
        with jax.named_scope("project"):
            send, keep = pl.pallas_call(
                functools.partial(project_kernel, tokens, sub),
                grid=(steps,),
                out_shape=[
                    shape((half, tokens, columns // chunks), BF16),
                    shape((half, tokens, columns // chunks), F32),
                ],
                in_specs=[SMEM]
                + [pl.BlockSpec((pieces, ratio, SPAN, width), lambda i: (0, 0, 0, 0))] * sub
                + [pl.BlockSpec((depth, tile), lambda i, first=chunk * steps: (0, i + first))],
                out_specs=[pl.BlockSpec((half, tokens, tile), lambda i: (0, 0, i))] * 2,
                scratch_shapes=[pltpu.VMEM((shard_tokens, depth), BF16)],
                compiler_params=params(),
                cost_estimate=pl.CostEstimate(flops=10**9, bytes_accessed=4 * 10**6, transcendentals=0),
            )(place, *gated, output_weight)
        stage = 0
        while True:
            pairs = [(here, here ^ (1 << stage)) for here in range(n_head)]
            arrived = lax.ppermute(send, "head", pairs)
            if keep.shape[0] == 1:
                summed.append((keep[0] + arrived[0].astype(F32)).astype(BF16))
                break
            stage += 1
            with jax.named_scope("halve"):
                left = (keep.shape[0] // 2,) + keep.shape[1:]
                send, keep = pl.pallas_call(
                    functools.partial(halve_kernel, stage),
                    out_shape=[shape(left, BF16), shape(left, F32)],
                    in_specs=[SMEM, VMEM, VMEM],
                    out_specs=[VMEM] * 2,
                    compiler_params=params(),
                )(place, keep, arrived)
    return jnp.concatenate(summed, axis=1)


def solution(mesh):
    n_seq, n_head = mesh.shape["seq"], mesh.shape["head"]

    def run(queries, key_vectors, value_vectors, output_gate, write_strength, norm_gain, output_weight):
        sub = queries.shape[1] // n_head
        outer = n_seq // sub
        split = Mesh(mesh.devices.reshape(outer, sub, n_head), ("outer", "sub", "head"))
        every = ("outer", "sub", "head")
        placed = (
            P(every, None, None),
            P(every, None, None),
            P(every, None, None),
            P(every, None, None),
            P(every, None),
            P(),
            P("head", None),
        )
        return jax.shard_map(
            functools.partial(per_device, outer, sub, n_head),
            mesh=split,
            in_specs=placed,
            out_specs=P(every, None),
            check_vma=False,
        )(queries, key_vectors, value_vectors, output_gate, write_strength, norm_gain, output_weight)

    return run
```

profile of v0, /device:TPU:0, one launch (start us, length us, event | category | flops | bytes accessed | tf_op | source)
XLA Modules:
  0.0 68.7 jit_solution(8055765531630206821)
XLA Ops:
  0.0 2.3 %pack_write.1 = bf16[16,208,128]{2,1,0:T(8,128)(2,1)} custom-call(bf16[64,16,128]{2,1,0:T(8,128)(2,1)} %k_hbm.1, bf16[64,32,128]{2,1,0:T(8,128)(2,1)} %v_hbm.1, bf16[32,64]{1,0:T(8,128)(2,1)} %bitcast.9), custom_call_target="tpu_custom_call" | custom-call | tf_op jit(solution)/shard_map/pack_write/pallas_call | solution.py:269
  2.3 6.3 %all-to-all-start = ((bf16[16,208,128]{2,1,0:T(8,128)(2,1)}), bf16[16,208,128]{2,1,0:T(8,128)(2,1)S(1)}, u32[]{:S(2)}, u32[]{:S(2)}) async-start(bf16[16,208,128]{2,1,0:T(8,128)(2,1)} %pack_write.1), calls=%async_computation | async-start | bytes 1703936 | tf_op jit(solution)/shard_map/all_to_all | solution.py:282
  8.6 2.2 %pack_read.1 = bf16[16,192,128]{2,1,0:T(8,128)(2,1)} custom-call(bf16[64,16,128]{2,1,0:T(8,128)(2,1)} %q_hbm.1, bf16[64,32,128]{2,1,0:T(8,128)(2,1)} %g_hbm.1), custom_call_target="tpu_custom_call" | custom-call | tf_op jit(solution)/shard_map/pack_read/pallas_call | solution.py:284
  10.8 11.9 %all-to-all-done.got_ref = bf16[16,208,128]{2,1,0:T(8,128)(2,1)S(1)} async-done(((bf16[16,208,128]{2,1,0:T(8,128)(2,1)}), bf16[16,208,128]{2,1,0:T(8,128)(2,1)S(1)}, u32[]{:S(2)}, u32[]{:S(2)}) %all-to-all-start) | async-done | bytes 852000 | tf_op jit(solution)/shard_map/all_to_all | solution.py:282
  22.7 3.6 %all-to-all-start.1 = ((bf16[16,192,128]{2,1,0:T(8,128)(2,1)}), bf16[16,192,128]{2,1,0:T(8,128)(2,1)S(1)}, u32[]{:S(2)}, u32[]{:S(2)}) async-start(bf16[16,192,128]{2,1,0:T(8,128)(2,1)} %pack_read.1), calls=%async_computation.1 | async-start | bytes 1572864 | tf_op jit(solution)/shard_map/all_to_all | solution.py:296
  26.3 0.1 pad_add_fusion.place_ref
  26.4 3.8 %factors.1 = (bf16[2,128,128]{2,1,0:T(8,128)(2,1)S(1)}, bf16[8,2,128,128]{3,2,1,0:T(8,128)(2,1)S(1)}, f32[8,2,128,128]{3,2,1,0:T(8,128)S(1)}, bf16[8,2,128,128]{...) custom-call(bf16[16,208,128]{2,1,0:T(8,128)(2,1)S(1)} %all-to-all-done.got_ref), custom_call_target="tpu_custom_call" | custom-call | flops 5000000000 | bytes 4000000 | tf_op jit(solution)/shard_map/factors/pallas_call | solution.py:301
  30.2 0.8 %copy-done.1 = bf16[8,2,128,128]{3,2,1,0:T(8,128)(2,1)} copy-done((bf16[8,2,128,128]{3,2,1,0:T(8,128)(2,1)}, bf16[8,2,128,128]{3,2,1,0:T(8,128)(2,1)S(1)}, u32[]{:S(2)}) %copy-start.1) | copy-done | bytes 524312
  31.0 0.8 %copy-done.3 = bf16[8,2,128,128]{3,2,1,0:T(8,128)(2,1)} copy-done((bf16[8,2,128,128]{3,2,1,0:T(8,128)(2,1)}, bf16[8,2,128,128]{3,2,1,0:T(8,128)(2,1)S(1)}, u32[]{:S(2)}) %copy-start.3) | copy-done | bytes 524312
  31.8 4.6 %collective-permute-start = (bf16[2,128,128]{2,1,0:T(8,128)(2,1)S(1)}, bf16[2,128,128]{2,1,0:T(8,128)(2,1)S(1)}, u32[]{:S(2)}, u32[]{:S(2)}) collective-permute-start(bf16[2,128,128]{2,1,0:T(8,128)(2,1)S(1)} %get-tuple-element.24), channel_id=1, source_target_pairs={{0,16},{1,17},{2,18},{3,19},{4,20},{5,21},{6,22},{7,23},{8,24},{9,... | collective-permute-start | bytes 196616 | tf_op jit(solution)/shard_map/ppermute | solution.py:318
  36.4 3.2 %all-to-all-done.1.read_ref = bf16[16,192,128]{2,1,0:T(8,128)(2,1)S(1)} async-done(((bf16[16,192,128]{2,1,0:T(8,128)(2,1)}), bf16[16,192,128]{2,1,0:T(8,128)(2,1)S(1)}, u32[]{:S(2)}, u32[]{:S(2)}) %all-to-all-start.1) | async-done | bytes 786464 | tf_op jit(solution)/shard_map/all_to_all | solution.py:296
  39.7 1.2 %copy-done.2 = bf16[8,2,128,128]{3,2,1,0:T(8,128)(2,1)S(1)} copy-done((bf16[8,2,128,128]{3,2,1,0:T(8,128)(2,1)S(1)}, bf16[8,2,128,128]{3,2,1,0:T(8,128)(2,1)}, u32[]{:S(2)}) %copy-start.2) | copy-done | bytes 524312
  40.9 1.3 %copy-done.4 = bf16[8,2,128,128]{3,2,1,0:T(8,128)(2,1)S(1)} copy-done((bf16[8,2,128,128]{3,2,1,0:T(8,128)(2,1)S(1)}, bf16[8,2,128,128]{3,2,1,0:T(8,128)(2,1)}, u32[]{:S(2)}) %copy-start.4) | copy-done | bytes 524312
  42.2 2.3 %spread.1 = (f32[2,8,128,128]{3,2,1,0:T(8,128)S(1)}, bf16[2,8,128,128]{3,2,1,0:T(8,128)(2,1)S(1)}, f32[2,128,128]{2,1,0:T(8,128)}) custom-call(bf16[16,208,128]{2,1,0:T(8,128)(2,1)S(1)} %all-to-all-done.got_ref, bf16[16,192,128]{2,1,0:T(8,128)(2,1)S(1)} %all-to-all-done.1.read_ref, bf16[8,2,128,128]{3,2,1,0:T(8,128)(2,1)S(1)} %get-tuple-element.25.w_ref, ...), custom_call_target="tpu_custom_call" | custom-call | flops 1000000000 | bytes 8000000 | tf_op jit(solution)/shard_map/spread/pallas_call | solution.py:320
  44.4 1.3 %join.1 = (bf16[2,2,128,128]{3,2,1,0:T(8,128)(2,1)S(1)}, bf16[2,2,128,128]{3,2,1,0:T(8,128)(2,1)S(1)}, bf16[2,2,128,128]{3,2,1,0:T(8,128)(2,1)S(1)}, bf16[2,2,128,128]{3,2,1,0:T(8,128)(2,1)S(1)}) custom-call(s32[2]{0:T(128)S(1)} %pad_add_fusion.place_ref, bf16[2,128,128]{2,1,0:T(8,128)(2,1)S(1)} %collective-permute-done.state_ref, ...), custom_call_target="tpu_custom_call" | custom-call | tf_op jit(solution)/shard_map/join/pallas_call | solution.py:338
  45.8 0.6 collective-permute-start.2
  46.4 2.9 %collective-permute-start.3 = (bf16[2,2,128,128]{3,2,1,0:T(8,128)(2,1)S(1)}, bf16[2,2,128,128]{3,2,1,0:T(8,128)(2,1)S(1)}, u32[]{:S(2)}, u32[]{:S(2)}) collective-permute-start(bf16[2,2,128,128]{3,2,1,0:T(8,128)(2,1)S(1)} %get-tuple-element.34), channel_id=1, source_target_pairs={{0,12},{4,8},{8,4},{12,0},{1,13},{5,9},{9,5},{13,1},{2,14},{6,10},... | collective-permute-start | bytes 393224 | tf_op jit(solution)/shard_map/ppermute | solution.py:348
  49.3 2.0 %collective-permute-done.1.refs_1_ = bf16[2,2,128,128]{3,2,1,0:T(8,128)(2,1)S(1)} collective-permute-done((bf16[2,2,128,128]{3,2,1,0:T(8,128)(2,1)S(1)}, bf16[2,2,128,128]{3,2,1,0:T(8,128)(2,1)S(1)}, u32[]{:S(2)}, u32[]{:S(2)}) %collective-permute-start.1) | collective-permute-done | bytes 131104 | tf_op jit(solution)/shard_map/ppermute | solution.py:348
  51.3 1.0 %collective-permute-done.2.refs_2_ = bf16[2,2,128,128]{3,2,1,0:T(8,128)(2,1)S(1)} collective-permute-done((bf16[2,2,128,128]{3,2,1,0:T(8,128)(2,1)S(1)}, bf16[2,2,128,128]{3,2,1,0:T(8,128)(2,1)S(1)}, u32[]{:S(2)}, u32[]{:S(2)}) %collective-permute-start.2) | collective-permute-done | bytes 131104 | tf_op jit(solution)/shard_map/ppermute | solution.py:348
  52.3 2.5 %collective-permute-done.3.refs_3_ = bf16[2,2,128,128]{3,2,1,0:T(8,128)(2,1)S(1)} collective-permute-done((bf16[2,2,128,128]{3,2,1,0:T(8,128)(2,1)S(1)}, bf16[2,2,128,128]{3,2,1,0:T(8,128)(2,1)S(1)}, u32[]{:S(2)}, u32[]{:S(2)}) %collective-permute-start.3) | collective-permute-done | bytes 131104 | tf_op jit(solution)/shard_map/ppermute | solution.py:348
  54.8 1.8 %project.2 = (bf16[2,64,1024]{2,1,0:T(8,128)(2,1)S(1)}, f32[2,64,1024]{2,1,0:T(8,128)S(1)}) custom-call(s32[2]{0:T(128)S(1)} %pad_add_fusion.place_ref, bf16[2,2,128,128]{3,2,1,0:T(8,128)(2,1)S(1)} %get-tuple-element.31.refs_0_, bf16[2,2,128,128]{3,2,1,0:T(8,128)(2,1)S(1)} %collective-permute-done.1.refs_1_, ...), custom_call_target="tpu_custom_call" | custom-call | flops 1000000000 | bytes 4000000 | tf_op jit(solution)/shard_map/project/pallas_call | solution.py:359
  56.6 0.1 collective-permute-start.4
  56.7 1.8 %project.3 = (bf16[2,64,1024]{2,1,0:T(8,128)(2,1)S(1)}, f32[2,64,1024]{2,1,0:T(8,128)S(1)}) custom-call(s32[2]{0:T(128)S(1)} %pad_add_fusion.place_ref, bf16[2,2,128,128]{3,2,1,0:T(8,128)(2,1)S(1)} %get-tuple-element.31.refs_0_, bf16[2,2,128,128]{3,2,1,0:T(8,128)(2,1)S(1)} %collective-permute-done.1.refs_1_, ...), custom_call_target="tpu_custom_call" | custom-call | flops 1000000000 | bytes 4000000 | tf_op jit(solution)/shard_map/project/pallas_call | solution.py:359
  58.5 0.5 collective-permute-start.6
  59.0 0.6 halve.2
  59.6 0.3 collective-permute-start.5
  59.9 0.3 collective-permute-done.6.got_ref
  60.2 0.6 halve.3
  60.8 1.6 %collective-permute-start.7 = (bf16[1,64,1024]{2,1,0:T(8,128)(2,1)S(1)}, bf16[1,64,1024]{2,1,0:T(8,128)(2,1)S(1)}, u32[]{:S(2)}, u32[]{:S(2)}) collective-permute-start(bf16[1,64,1024]{2,1,0:T(8,128)(2,1)S(1)} %get-tuple-element.42), channel_id=1, source_target_pairs={{0,2},{1,3},{2,0},{3,1},{4,6},{5,7},{6,4},{7,5},{8,10},{9,11},{10,... | collective-permute-start | bytes 393224 | tf_op jit(solution)/shard_map/ppermute | solution.py:377
  62.4 3.7 %collective-permute-done.5 = bf16[1,64,1024]{2,1,0:T(8,128)(2,1)S(1)} collective-permute-done((bf16[1,64,1024]{2,1,0:T(8,128)(2,1)S(1)}, bf16[1,64,1024]{2,1,0:T(8,128)(2,1)S(1)}, u32[]{:S(2)}, u32[]{:S(2)}) %collective-permute-start.5) | collective-permute-done | bytes 131104 | tf_op jit(solution)/shard_map/ppermute | solution.py:377
  66.1 1.9 %collective-permute-done.7 = bf16[1,64,1024]{2,1,0:T(8,128)(2,1)S(1)} collective-permute-done((bf16[1,64,1024]{2,1,0:T(8,128)(2,1)S(1)}, bf16[1,64,1024]{2,1,0:T(8,128)(2,1)S(1)}, u32[]{:S(2)}, u32[]{:S(2)}) %collective-permute-start.7) | collective-permute-done | bytes 131104 | tf_op jit(solution)/shard_map/ppermute | solution.py:377
  67.9 0.7 %pad_maximum_fusion = bf16[64,2048]{1,0:T(8,128)(2,1)} fusion(bf16[64,1024]{1,0:T(8,128)(2,1)S(1)} %fusion.1, bf16[64,1024]{1,0:T(8,128)(2,1)S(1)} %fusion), kind=kLoop, calls=%fused_computation | loop fusion | flops 524288 | bytes 524288 | tf_op jit(solution)/shard_map/concatenate | solution.py:391
  (13 shorter events, 0.1 us)
Async XLA Ops:
  2.3 20.4 %all-to-all-start = ((bf16[16,208,128]{2,1,0:T(8,128)(2,1)}), bf16[16,208,128]{2,1,0:T(8,128)(2,1)S(1)}, u32[]{:S(2)}, u32[]{:S(2)}) async-start(bf16[16,208,128]{2,1,0:T(8,128)(2,1)} %pack_write.1), calls=%async_computation | async-start | bytes 1703936 | tf_op jit(solution)/shard_map/all_to_all | solution.py:282
  22.7 17.0 %all-to-all-start.1 = ((bf16[16,192,128]{2,1,0:T(8,128)(2,1)}), bf16[16,192,128]{2,1,0:T(8,128)(2,1)S(1)}, u32[]{:S(2)}, u32[]{:S(2)}) async-start(bf16[16,192,128]{2,1,0:T(8,128)(2,1)} %pack_read.1), calls=%async_computation.1 | async-start | bytes 1572864 | tf_op jit(solution)/shard_map/all_to_all | solution.py:296
  30.2 0.8 %copy-start.1 = (bf16[8,2,128,128]{3,2,1,0:T(8,128)(2,1)}, bf16[8,2,128,128]{3,2,1,0:T(8,128)(2,1)S(1)}, u32[]{:S(2)}) copy-start(bf16[8,2,128,128]{3,2,1,0:T(8,128)(2,1)S(1)} %get-tuple-element.27.trans_ref) | copy-start | bytes 1572868
  31.0 0.8 %copy-start.3 = (bf16[8,2,128,128]{3,2,1,0:T(8,128)(2,1)}, bf16[8,2,128,128]{3,2,1,0:T(8,128)(2,1)S(1)}, u32[]{:S(2)}) copy-start(bf16[8,2,128,128]{3,2,1,0:T(8,128)(2,1)S(1)} %get-tuple-element.28.prefix_ref) | copy-start | bytes 1572868
  31.8 12.6 %copy-start.5 = (bf16[128]{0:T(256)(128)(2,1)S(1)}, bf16[128]{0:T(256)(128)(2,1)}, u32[]{:S(2)}) copy-start(bf16[128]{0:T(256)(128)(2,1)} %param.12) | copy-start | bytes 772
  31.8 12.6 %collective-permute-start = (bf16[2,128,128]{2,1,0:T(8,128)(2,1)S(1)}, bf16[2,128,128]{2,1,0:T(8,128)(2,1)S(1)}, u32[]{:S(2)}, u32[]{:S(2)}) collective-permute-start(bf16[2,128,128]{2,1,0:T(8,128)(2,1)S(1)} %get-tuple-element.24), channel_id=1, source_target_pairs={{0,16},{1,17},{2,18},{3,19},{4,20},{5,21},{6,22},{7,23},{8,24},{9,... | collective-permute-start | bytes 196616 | tf_op jit(solution)/shard_map/ppermute | solution.py:318
  39.7 15.1 %copy-start = (bf16[1024,2048]{1,0:T(8,128)(2,1)S(1)}, bf16[1024,2048]{1,0:T(8,128)(2,1)}, u32[]{:S(2)}) copy-start(bf16[1024,2048]{1,0:T(8,128)(2,1)} %refs_4_.3) | copy-start | bytes 12582916
  39.7 1.2 %copy-start.2 = (bf16[8,2,128,128]{3,2,1,0:T(8,128)(2,1)S(1)}, bf16[8,2,128,128]{3,2,1,0:T(8,128)(2,1)}, u32[]{:S(2)}) copy-start(bf16[8,2,128,128]{3,2,1,0:T(8,128)(2,1)} %copy-done.1) | copy-start | bytes 1572868
  40.9 1.3 %copy-start.4 = (bf16[8,2,128,128]{3,2,1,0:T(8,128)(2,1)S(1)}, bf16[8,2,128,128]{3,2,1,0:T(8,128)(2,1)}, u32[]{:S(2)}) copy-start(bf16[8,2,128,128]{3,2,1,0:T(8,128)(2,1)} %copy-done.3) | copy-start | bytes 1572868
  45.7 5.6 %collective-permute-start.1 = (bf16[2,2,128,128]{3,2,1,0:T(8,128)(2,1)S(1)}, bf16[2,2,128,128]{3,2,1,0:T(8,128)(2,1)S(1)}, u32[]{:S(2)}, u32[]{:S(2)}) collective-permute-start(bf16[2,2,128,128]{3,2,1,0:T(8,128)(2,1)S(1)} %get-tuple-element.32), channel_id=1, source_target_pairs={{0,4},{4,0},{8,12},{12,8},{1,5},{5,1},{9,13},{13,9},{2,6},{6,2},{1... | collective-permute-start | bytes 393224 | tf_op jit(solution)/shard_map/ppermute | solution.py:348
  45.8 6.5 %collective-permute-start.2 = (bf16[2,2,128,128]{3,2,1,0:T(8,128)(2,1)S(1)}, bf16[2,2,128,128]{3,2,1,0:T(8,128)(2,1)S(1)}, u32[]{:S(2)}, u32[]{:S(2)}) collective-permute-start(bf16[2,2,128,128]{3,2,1,0:T(8,128)(2,1)S(1)} %get-tuple-element.33), channel_id=1, source_target_pairs={{0,8},{4,12},{8,0},{12,4},{1,9},{5,13},{9,1},{13,5},{2,10},{6,14},... | collective-permute-start | bytes 393224 | tf_op jit(solution)/shard_map/ppermute | solution.py:348
  46.4 8.4 %collective-permute-start.3 = (bf16[2,2,128,128]{3,2,1,0:T(8,128)(2,1)S(1)}, bf16[2,2,128,128]{3,2,1,0:T(8,128)(2,1)S(1)}, u32[]{:S(2)}, u32[]{:S(2)}) collective-permute-start(bf16[2,2,128,128]{3,2,1,0:T(8,128)(2,1)S(1)} %get-tuple-element.34), channel_id=1, source_target_pairs={{0,12},{4,8},{8,4},{12,0},{1,13},{5,9},{9,5},{13,1},{2,14},{6,10},... | collective-permute-start | bytes 393224 | tf_op jit(solution)/shard_map/ppermute | solution.py:348
  56.6 2.4 %collective-permute-start.4 = (bf16[2,64,1024]{2,1,0:T(8,128)(2,1)S(1)}, bf16[2,64,1024]{2,1,0:T(8,128)(2,1)S(1)}, u32[]{:S(2)}, u32[]{:S(2)}) collective-permute-start(bf16[2,64,1024]{2,1,0:T(8,128)(2,1)S(1)} %get-tuple-element.36), channel_id=1, source_target_pairs={{0,1},{1,0},{2,3},{3,2},{4,5},{5,4},{6,7},{7,6},{8,9},{9,8},{10,11... | collective-permute-start | bytes 786440 | tf_op jit(solution)/shard_map/ppermute | solution.py:377
  58.5 1.7 %collective-permute-start.6 = (bf16[2,64,1024]{2,1,0:T(8,128)(2,1)S(1)}, bf16[2,64,1024]{2,1,0:T(8,128)(2,1)S(1)}, u32[]{:S(2)}, u32[]{:S(2)}) collective-permute-start(bf16[2,64,1024]{2,1,0:T(8,128)(2,1)S(1)} %get-tuple-element.40), channel_id=1, source_target_pairs={{0,1},{1,0},{2,3},{3,2},{4,5},{5,4},{6,7},{7,6},{8,9},{9,8},{10,11... | collective-permute-start | bytes 786440 | tf_op jit(solution)/shard_map/ppermute | solution.py:377
  59.6 6.4 %collective-permute-start.5 = (bf16[1,64,1024]{2,1,0:T(8,128)(2,1)S(1)}, bf16[1,64,1024]{2,1,0:T(8,128)(2,1)S(1)}, u32[]{:S(2)}, u32[]{:S(2)}) collective-permute-start(bf16[1,64,1024]{2,1,0:T(8,128)(2,1)S(1)} %get-tuple-element.38), channel_id=1, source_target_pairs={{0,2},{1,3},{2,0},{3,1},{4,6},{5,7},{6,4},{7,5},{8,10},{9,11},{10,... | collective-permute-start | bytes 393224 | tf_op jit(solution)/shard_map/ppermute | solution.py:377
  60.8 7.2 %collective-permute-start.7 = (bf16[1,64,1024]{2,1,0:T(8,128)(2,1)S(1)}, bf16[1,64,1024]{2,1,0:T(8,128)(2,1)S(1)}, u32[]{:S(2)}, u32[]{:S(2)}) collective-permute-start(bf16[1,64,1024]{2,1,0:T(8,128)(2,1)S(1)} %get-tuple-element.42), channel_id=1, source_target_pairs={{0,2},{1,3},{2,0},{3,1},{4,6},{5,7},{6,4},{7,5},{8,10},{9,11},{10,... | collective-permute-start | bytes 393224 | tf_op jit(solution)/shard_map/ppermute | solution.py:377
where the time goes:
time: 69 us; the launch traced here: 68.7 us
  waiting for transfers between devices  26.5 us (38%)
  starting transfers between devices  20.6 us (30%)
  Pallas kernels  16.5 us (24%)
  local copies, waits for them, and re-layouts  4.06 us (6%)
  other arithmetic  0.85 us (1%)
    all_to_all x1, waiting for transfers between devices, per_device(): lax.all_to_all(write, ('sub', 'head'), split_axis=0, concat_axis=0, tiled...  11.9 us
    all_to_all x1, starting transfers between devices, per_device(): lax.all_to_all(write, ('sub', 'head'), split_axis=0, concat_axis=0, tiled...  6.3 us
    ppermute x4, waiting for transfers between devices, per_device(): arrived = lax.ppermute(send, 'head', pairs)  5.82 us
    ppermute x3, waiting for transfers between devices, per_device(): gated[distance] = lax.ppermute(gated[distance], 'sub', pairs)  5.54 us
    ppermute x1, starting transfers between devices, per_device(): incoming = lax.ppermute(state, 'outer', onward)  4.62 us
    unnamed x12, local copies, waits for them, and re-layouts  4.06 us
    pallas_call x1, Pallas kernels, per_device(): pl.pallas_call(functools.partial(factor_kernel, tokens, ratio, blocks), o...  3.79 us
    all_to_all x1, starting transfers between devices, per_device(): lax.all_to_all(read, ('sub', 'head'), split_axis=0, concat_axis=0, tiled=...  3.61 us
  transfers between devices with their start and end apart: 10, of which 8 were waited for; matrix products, arithmetic and copies ran while one was open for 0% of the time, Pallas kernels for 16%

commit v1 on v0

v1 whole, which is shorter than its diff:
```python
import functools

import jax
import jax.numpy as jnp
from jax import lax
from jax.experimental import pallas as pl
from jax.experimental.pallas import tpu as pltpu
from jax.sharding import Mesh, PartitionSpec as P

SPAN = 128
EPSILON = 1e-06
F32 = jnp.float32
BF16 = jnp.bfloat16
ROW_TILE = 16
VMEM = pl.BlockSpec(memory_space=pltpu.VMEM)
SMEM = pl.BlockSpec(memory_space=pltpu.SMEM)
ANY = pl.BlockSpec(memory_space=pl.ANY)


def dot(left, right):
    return jnp.dot(left, right, preferred_element_type=F32)


def dot_nt(left, right):
    return lax.dot_general(left, right, (((1,), (1,)), ((), ())), preferred_element_type=F32)


def params(megabytes=24):
    return pltpu.CompilerParams(vmem_limit_bytes=megabytes * 2**20)


def turned(values):
    return jnp.transpose(values, (1, 0, 2))


def pack_kernel(sub, place_ref, q_hbm, k_hbm, v_hbm, b_hbm, *refs):
    tokens, key_heads, width = q_hbm.shape
    ratio = v_hbm.shape[1] // key_heads
    n_head = key_heads // sub
    out_refs = refs[:key_heads]
    q_ref, k_ref, v_ref, b_ref, q_turned, k_turned, v_turned, b_turned, done = refs[key_heads:]
    copies = [
        pltpu.make_async_copy(source, target, done.at[number])
        for number, (source, target) in enumerate(
            ((b_hbm, b_ref), (k_hbm, k_ref), (q_hbm, q_ref), (v_hbm, v_ref))
        )
    ]
    for copy in copies:
        copy.start()
    copies[0].wait()
    strength = jnp.concatenate([b_ref[...].astype(F32)] * (width // tokens), axis=1)
    strength = jnp.concatenate([strength, jnp.zeros((ROW_TILE, width), F32)], axis=0)
    for head in range(key_heads):
        b_turned[head] = strength[head * ratio : head * ratio + ROW_TILE].astype(BF16)
    for copy, source, target in zip(copies[1:], (k_ref, q_ref, v_ref), (k_turned, q_turned, v_turned)):
        copy.wait()
        target[...] = turned(source[...])
    mine = place_ref[0] * n_head + place_ref[1]
    for distance, out_ref in enumerate(out_refs):
        peer = mine ^ distance
        head = (peer % n_head) * sub + peer // n_head
        out_ref[0:tokens] = q_turned[head]
        out_ref[tokens : 2 * tokens] = k_turned[head]
        for r in range(ratio):
            out_ref[(2 + r) * tokens : (3 + r) * tokens] = v_turned[head * ratio + r]
        out_ref[(2 + ratio) * tokens :] = b_turned[head]


def gate_kernel(place_ref, gate_ref, gain_ref, unused_ref, *refs):
    out_refs, gates = refs[:-1], refs[-1]
    gate = gate_ref[...].astype(F32)
    gated = gain_ref[...].astype(F32)[:, None] * (gate / (1.0 + jnp.exp(-gate)))
    gates[...] = turned(gated.astype(BF16))
    for distance, out_ref in enumerate(out_refs):
        heads = out_ref.shape[0]
        out_ref[...] = gates[pl.ds((place_ref[1] ^ distance) * heads, heads)]


def block_rows(got_ref, block, per, tokens, part):
    rows = got_ref[pl.ds(block * per, per), part * tokens : (part + 1) * tokens]
    return rows.reshape(per * tokens, rows.shape[-1])


def block_inverse(below):
    size = below[0].shape[0]
    rows = lax.broadcasted_iota(jnp.int32, (size, size), 0)
    cols = lax.broadcasted_iota(jnp.int32, (size, size), 1)
    zero = jnp.zeros((size, size), F32)
    step = 1
    solved = None
    while step < size:
        joins = (rows // (2 * step) == cols // (2 * step)) & (rows // step > cols // step)
        parts = [jnp.where(joins, matrix, zero) for matrix in below]
        if step == 1:
            solved = [
                jnp.where(rows == cols, jnp.ones_like(zero), -part).astype(BF16) for part in parts
            ]
        else:
            inner = [dot(part.astype(BF16), now).astype(BF16) for part, now in zip(parts, solved)]
            solved = [now - dot(now, mid).astype(BF16) for now, mid in zip(solved, inner)]
        step *= 2
    return solved


def factor_kernel(tokens, ratio, n_head, place_ref, *refs):
    sources = len(refs) - 7
    slab_refs = refs[:sources]
    got_ref, state_ref, w_ref, u_ref, trans_ref, prefix_ref, add_ref = refs[sources:]
    mine = place_ref[0] * n_head + place_ref[1]
    for distance, slab_ref in enumerate(slab_refs):
        got_ref[mine ^ distance] = slab_ref[...]

    width = got_ref.shape[-1]
    per = SPAN // tokens
    blocks = got_ref.shape[0] // per
    rows = lax.broadcasted_iota(jnp.int32, (SPAN, SPAN), 0)
    cols = lax.broadcasted_iota(jnp.int32, (SPAN, SPAN), 1)
    lane = lax.broadcasted_iota(jnp.int32, (1, SPAN), 1)
    first = (2 + ratio) * tokens
    below, held = [], []
    for block in range(blocks):
        key = block_rows(got_ref, block, per, tokens, 1)
        gram = dot_nt(key, key)
        squares = jnp.where(rows == cols, gram, 0.0)
        key_row = lax.rsqrt(jnp.sum(squares, 0, keepdims=True) + EPSILON)
        key_col = lax.rsqrt(jnp.sum(squares, 1, keepdims=True) + EPSILON)
        lower = jnp.where(rows > cols, gram, 0.0) * key_row
        for r in range(ratio):
            strength = jnp.zeros((1, SPAN), F32)
            for place in range(per):
                piece = got_ref[block * per + place, first : first + ROW_TILE].astype(F32)[r : r + 1]
                strength = jnp.where(lane // tokens == place, piece, strength)
            scaled_col = jnp.sum(jnp.where(rows == cols, strength * key_row, 0.0), 1, keepdims=True)
            below.append(lower * scaled_col)
            held.append((block, r, key, key_col, key_row, strength))
    solved = block_inverse(below)
    for now, (block, r, key, key_col, key_row, strength) in zip(solved, held):
        value = block_rows(got_ref, block, per, tokens, 2 + r)
        weighted = now.astype(F32) * key_col * strength
        u_now = dot(weighted.astype(BF16), value)
        w_now = dot((weighted * key_row).astype(BF16), key).astype(BF16)
        both = dot(key.T, jnp.concatenate([w_now, u_now.astype(BF16)], axis=1))
        w_ref[block, r] = w_now
        u_ref[block, r] = u_now
        trans_ref[block, r] = both[:, :width].astype(BF16)
        add_ref[block, r] = both[:, width:]

    states = [jnp.zeros((width, width), F32) for r in range(ratio)]
    for block in range(blocks):
        for r in range(ratio):
            held = states[r].astype(BF16)
            prefix_ref[block, r] = held
            if block == 0:
                states[r] = add_ref[block, r]
            else:
                states[r] = states[r] + add_ref[block, r] - dot(trans_ref[block, r], held)
    for r in range(ratio):
        state_ref[r] = states[r].astype(state_ref.dtype)


def spread_kernel(
    tokens, ratio, got_ref, w_ref, u_ref, trans_ref, prefix_ref, local_ref, reach_ref, total_ref
):
    width = got_ref.shape[-1]
    per = SPAN // tokens
    blocks = got_ref.shape[0] // per
    rows = lax.broadcasted_iota(jnp.int32, (SPAN, SPAN), 0)
    cols = lax.broadcasted_iota(jnp.int32, (SPAN, SPAN), 1)
    wide_rows = lax.broadcasted_iota(jnp.int32, (width, width), 0)
    wide_cols = lax.broadcasted_iota(jnp.int32, (width, width), 1)
    identity = jnp.where(wide_rows == wide_cols, 1.0, 0.0).astype(F32)
    carried = [identity for r in range(ratio)]
    for block in range(blocks):
        query = block_rows(got_ref, block, per, tokens, 0)
        key = block_rows(got_ref, block, per, tokens, 1)
        scores = jnp.where(rows >= cols, dot_nt(query, key), 0.0).astype(BF16)
        query_f = query.astype(F32)
        squares = jnp.sum(query_f * query_f, 1, keepdims=True)
        unit = lax.rsqrt(squares + EPSILON) * width ** (-0.5)
        left = jnp.concatenate([query, scores], axis=1)
        for r in range(ratio):
            held = carried[r].astype(BF16)
            if block == 0:
                carried[r] = identity - trans_ref[block, r].astype(F32)
            else:
                carried[r] = carried[r] - dot(trans_ref[block, r], held)
            starts = jnp.concatenate([prefix_ref[block, r], held], axis=1)
            passed = dot(w_ref[block, r], starts)
            corrected = jnp.concatenate([u_ref[block, r] - passed[:, :width], -passed[:, width:]], axis=1)
            right = jnp.concatenate([starts, corrected.astype(BF16)], axis=0)
            out = dot(left, right) * unit
            local_ref[r, block] = out[:, :width]
            reach_ref[r, block] = out[:, width:].astype(BF16)
    for r in range(ratio):
        total_ref[r] = carried[r]


def join_kernel(place_ref, state_ref, local_ref, reach_ref, *out_refs):
    ratio, blocks, span, width = local_ref.shape
    pieces = blocks // len(out_refs)
    for distance, out_ref in enumerate(out_refs):
        target = place_ref[0] ^ distance
        for piece in range(pieces):
            block = target * pieces + piece
            for r in range(ratio):
                core = local_ref[r, block] + dot(reach_ref[r, block], state_ref[r].astype(BF16))
                mean_square = jnp.mean(core * core, 1, keepdims=True)
                out_ref[piece, r] = (core * lax.rsqrt(mean_square + EPSILON)).astype(BF16)


def project(chunk, rows, weight_ref, send_ref, keep_ref):
    half, tokens, columns = keep_ref.shape
    out = dot(rows, weight_ref[:, chunk * columns : (chunk + 1) * columns]).reshape(2, half, tokens, columns)
    send_ref[...] = out[0].astype(BF16)
    keep_ref[...] = out[1]


def project_kernel(parts, chunk, place_ref, *refs):
    normed_refs, gate_refs, (weight_ref, send_ref, keep_ref, rows_ref) = refs[:parts], refs[parts:-4], refs[-4:]
    pieces, ratio, span, width = normed_refs[0].shape
    tokens = gate_refs[0].shape[1]
    per = span // tokens
    half = len(gate_refs) // 2
    for distance, normed_ref in enumerate(normed_refs):
        source = place_ref[0] ^ distance
        for apart, gate_ref in enumerate(gate_refs):
            share = place_ref[1] ^ apart
            first = ((1 - apart % 2) * half + share // 2) * tokens
            place = pl.ds(pl.multiple_of(first, tokens), tokens)
            from_rows = pl.ds(pl.multiple_of(share % per * tokens, tokens), tokens)
            for r in range(ratio):
                lanes = pl.ds(pl.multiple_of((source * ratio + r) * width, width), width)
                normed = normed_ref[share // per, r, from_rows].astype(F32)
                gate = gate_ref[source * ratio + r].astype(F32)
                rows_ref[place, lanes] = (normed * gate).astype(BF16)
    project(chunk, rows_ref[...], weight_ref, send_ref, keep_ref)


def project_more_kernel(chunk, rows_ref, weight_ref, send_ref, keep_ref):
    project(chunk, rows_ref[...], weight_ref, send_ref, keep_ref)


def halve_kernel(stage, place_ref, keep_ref, got_ref, send_ref, left_ref):
    bit = (place_ref[1] >> stage) & 1
    for place in range(keep_ref.shape[0] // 2):
        there, here = 2 * place + 1 - bit, 2 * place + bit
        send_ref[place] = (keep_ref[there] + got_ref[there].astype(F32)).astype(BF16)
        left_ref[place] = keep_ref[here] + got_ref[here].astype(F32)


def finish_kernel(*refs):
    out_ref = refs[-1]
    keep_refs, got_refs = refs[: len(refs) // 2], refs[len(refs) // 2 : -1]
    first = 0
    for keep_ref, got_ref in zip(keep_refs, got_refs):
        columns = keep_ref.shape[-1]
        out_ref[:, first : first + columns] = (keep_ref[0] + got_ref[0].astype(F32)).astype(BF16)
        first += columns


def per_device(
    outer, sub, n_head, queries, key_vectors, value_vectors, output_gate, write_strength, norm_gain, output_weight
):
    tokens, key_heads, width = queries.shape
    value_heads = value_vectors.shape[1]
    ratio = value_heads // key_heads
    sources = sub * n_head
    shard = tokens * sources
    blocks = shard // SPAN
    shard_tokens = tokens * n_head
    shape = jax.ShapeDtypeStruct
    place = jnp.stack([lax.axis_index("sub"), lax.axis_index("head")]).astype(jnp.int32)

    with jax.named_scope("pack"):
        slab = shape(((2 + ratio) * tokens + ROW_TILE, width), BF16)
        slabs = pl.pallas_call(
            functools.partial(pack_kernel, sub),
            out_shape=[slab] * sources,
            in_specs=[SMEM] + [ANY] * 4,
            out_specs=[VMEM] * sources,
            scratch_shapes=[
                pltpu.VMEM(queries.shape, BF16),
                pltpu.VMEM(key_vectors.shape, BF16),
                pltpu.VMEM(value_vectors.shape, BF16),
                pltpu.VMEM((value_heads, tokens), BF16),
                pltpu.VMEM((key_heads, tokens, width), BF16),
                pltpu.VMEM((key_heads, tokens, width), BF16),
                pltpu.VMEM((value_heads, tokens, width), BF16),
                pltpu.VMEM((key_heads, ROW_TILE, width), BF16),
                pltpu.SemaphoreType.DMA((4,)),
            ],
            compiler_params=params(60),
        )(place, queries, key_vectors, value_vectors, write_strength.T)
    slabs = list(slabs)
    for distance in reversed(range(1, sources)):
        pairs = [(here, here ^ distance) for here in range(sources)]
        slabs[distance] = lax.ppermute(slabs[distance], ("sub", "head"), pairs)

    state_type = BF16 if outer == 2 else F32
    square = (blocks, ratio, width, width)
    with jax.named_scope("factors"):
        got, state, w, u, trans, prefix = pl.pallas_call(
            functools.partial(factor_kernel, tokens, ratio, n_head),
            out_shape=[
                shape((sources,) + slab.shape, BF16),
                shape((ratio, width, width), state_type),
                shape((blocks, ratio, SPAN, width), BF16),
                shape((blocks, ratio, SPAN, width), F32),
                shape(square, BF16),
                shape(square, BF16),
            ],
            in_specs=[SMEM] + [VMEM] * sources,
            out_specs=[VMEM] * 6,
            scratch_shapes=[pltpu.VMEM(square, F32)],
            compiler_params=params(),
            cost_estimate=pl.CostEstimate(flops=4 * 10**9, bytes_accessed=4 * 10**6, transcendentals=0),
        )(place, *slabs)

    onward = [(here, here + 1) for here in range(outer - 1)]
    incoming = lax.ppermute(state, "outer", onward)
    with jax.named_scope("spread"):
        local, reach, total = pl.pallas_call(
            functools.partial(spread_kernel, tokens, ratio),
            out_shape=[
                shape((ratio, blocks, SPAN, width), F32),
                shape((ratio, blocks, SPAN, width), BF16),
                shape((ratio, width, width), F32),
            ],
            in_specs=[VMEM] * 5,
            out_specs=[VMEM] * 3,
            compiler_params=params(),
            cost_estimate=pl.CostEstimate(flops=2 * 10**9, bytes_accessed=8 * 10**6, transcendentals=0),
        )(got, w, u, trans, prefix)
    heads = sub * ratio
    with jax.named_scope("gates"):
        gates = pl.pallas_call(
            gate_kernel,
            out_shape=[shape((heads, tokens, width), BF16)] * n_head,
            in_specs=[SMEM, VMEM, VMEM, ANY],
            out_specs=[VMEM] * n_head,
            scratch_shapes=[pltpu.VMEM((value_heads, tokens, width), BF16)],
            compiler_params=params(),
            cost_estimate=pl.CostEstimate(flops=10**9, bytes_accessed=8 * 10**6, transcendentals=0),
        )(place, output_gate, norm_gain.reshape(1, width), state)
    gates = list(gates)
    for distance in reversed(range(1, n_head)):
        pairs = [(here, here ^ distance) for here in range(n_head)]
        gates[distance] = lax.ppermute(gates[distance], "head", pairs)
    for hop in range(outer - 2):
        passed = jnp.einsum("hde,hef->hdf", total, incoming, precision=lax.Precision.HIGHEST)
        incoming = lax.ppermute(state + passed, "outer", onward)

    pieces = shard_tokens // SPAN
    with jax.named_scope("join"):
        normed = pl.pallas_call(
            join_kernel,
            out_shape=[shape((pieces, ratio, SPAN, width), BF16)] * sub,
            in_specs=[SMEM] + [VMEM] * 3,
            out_specs=[VMEM] * sub,
            compiler_params=params(),
        )(place, incoming, local, reach)
    normed = list(normed)
    for distance in reversed(range(1, sub)):
        pairs = [(here, here ^ distance) for here in range(sub)]
        normed[distance] = lax.ppermute(normed[distance], "sub", pairs)

    chunks = 2
    columns = output_weight.shape[1] // chunks
    half = n_head // 2
    out_shape = [shape((half, tokens, columns), BF16), shape((half, tokens, columns), F32)]
    kept, arrivals, rows = [], [], None
    for chunk in range(chunks):
        cost = pl.CostEstimate(flops=10**9, bytes_accessed=4 * 10**6, transcendentals=0)
        with jax.named_scope("project"):
            if chunk == 0:
                send, keep, rows = pl.pallas_call(
                    functools.partial(project_kernel, sub, chunk),
                    out_shape=out_shape + [shape((shard_tokens, heads * width), BF16)],
                    in_specs=[SMEM] + [VMEM] * (sub + n_head + 1),
                    out_specs=[VMEM] * 3,
                    compiler_params=params(),
                    cost_estimate=cost,
                )(place, *normed, *gates, output_weight)
            else:
                send, keep = pl.pallas_call(
                    functools.partial(project_more_kernel, chunk),
                    out_shape=out_shape,
                    in_specs=[VMEM] * 2,
                    out_specs=[VMEM] * 2,
                    compiler_params=params(),
                    cost_estimate=cost,
                )(rows, output_weight)
        stage = 0
        while True:
            pairs = [(here, here ^ (1 << stage)) for here in range(n_head)]
            arrived = lax.ppermute(send, "head", pairs)
            if keep.shape[0] == 1:
                kept.append(keep)
                arrivals.append(arrived)
                break
            stage += 1
            with jax.named_scope("halve"):
                left = (keep.shape[0] // 2,) + keep.shape[1:]
                send, keep = pl.pallas_call(
                    functools.partial(halve_kernel, stage),
                    out_shape=[shape(left, BF16), shape(left, F32)],
                    in_specs=[SMEM, VMEM, VMEM],
                    out_specs=[VMEM] * 2,
                    compiler_params=params(),
                )(place, keep, arrived)
    with jax.named_scope("finish"):
        return pl.pallas_call(
            finish_kernel,
            out_shape=shape((tokens, output_weight.shape[1]), BF16),
            in_specs=[VMEM] * (2 * chunks),
            out_specs=VMEM,
            compiler_params=params(),
        )(*kept, *arrivals)


def solution(mesh):
    n_seq, n_head = mesh.shape["seq"], mesh.shape["head"]

    def run(queries, key_vectors, value_vectors, output_gate, write_strength, norm_gain, output_weight):
        sub = queries.shape[1] // n_head
        outer = n_seq // sub
        split = Mesh(mesh.devices.reshape(outer, sub, n_head), ("outer", "sub", "head"))
        every = ("outer", "sub", "head")
        placed = (
            P(every, None, None),
            P(every, None, None),
            P(every, None, None),
            P(every, None, None),
            P(every, None),
            P(),
            P("head", None),
        )
        return jax.shard_map(
            functools.partial(per_device, outer, sub, n_head),
            mesh=split,
            in_specs=placed,
            out_specs=P(every, None),
            check_vma=False,
        )(queries, key_vectors, value_vectors, output_gate, write_strength, norm_gain, output_weight)

    return run
```

time: 69 us -> 68.7 us (level)
  starting transfers between devices: 20.6 us -> 31.7 us
  waiting for transfers between devices: 26.5 us -> 18.4 us
  local copies, waits for them, and re-layouts: 4.06 us -> 1.56 us
    ppermute x3 -> x21, starting transfers between devices: 3.55 us -> 24.4 us  [the longest x15 18.9 us: per_device(): slabs[distance] = lax.ppermute(slabs[distance], ('sub', 'head'), pairs)]
    all_to_all x2 -> x0, waiting for transfers between devices: 15.1 us -> none  [the longest x1 11.9 us: per_device(): lax.all_to_all(write, ('sub', 'head'), split_axis=0, concat_axis=0, tiled...]
    all_to_all x2 -> x0, starting transfers between devices: 9.91 us -> none  [the longest x1 6.3 us: per_device(): lax.all_to_all(write, ('sub', 'head'), split_axis=0, concat_axis=0, tiled...]
    ppermute x3 -> x21, waiting for transfers between devices: 5.54 us -> 12.5 us  [the longest x3 6.24 us: per_device(): normed[distance] = lax.ppermute(normed[distance], 'sub', pairs)]
    unnamed x12, local copies, waits for them, and re-layouts: 4.06 us -> 1.56 us
    concatenate x1 -> x0, other arithmetic: 0.72 us -> none  [per_device(): return jnp.concatenate(summed, axis=1)]
    pallas_call x6 -> x7, Pallas kernels: 13.1 us -> 12.6 us  [the longest x1 4.41 us: per_device(): pl.pallas_call(functools.partial(factor_kernel, tokens, ratio, n_head), o...]
  transfers between devices with their start and end apart: 10 -> 26, of which waited for: 8 -> 12; matrix products, arithmetic and copies ran while one was open for 0% -> 0% of each run, Pallas kernels for 16% -> 9%
where the time goes in v1:
time: 68.7 us; the launch traced here: 68.5 us
  starting transfers between devices  31.7 us (46%)
  waiting for transfers between devices  18.4 us (27%)
  Pallas kernels  16 us (23%)
  local copies, waits for them, and re-layouts  1.56 us (2%)
    ppermute x15, starting transfers between devices, per_device(): slabs[distance] = lax.ppermute(slabs[distance], ('sub', 'head'), pairs)  18.9 us
    ppermute x3, waiting for transfers between devices, per_device(): normed[distance] = lax.ppermute(normed[distance], 'sub', pairs)  6.24 us
    ppermute x15, waiting for transfers between devices, per_device(): slabs[distance] = lax.ppermute(slabs[distance], ('sub', 'head'), pairs)  6.23 us
    ppermute x4, waiting for transfers between devices, per_device(): arrived = lax.ppermute(send, 'head', pairs)  5.91 us
    ppermute x1, starting transfers between devices, per_device(): incoming = lax.ppermute(state, 'outer', onward)  4.5 us
    pallas_call x1, Pallas kernels, per_device(): pl.pallas_call(functools.partial(factor_kernel, tokens, ratio, n_head), o...  4.41 us
    ppermute x3, starting transfers between devices, per_device(): normed[distance] = lax.ppermute(normed[distance], 'sub', pairs)  3.55 us
    pallas_call x1, Pallas kernels, per_device(): pl.pallas_call(functools.partial(pack_kernel, sub), out_shape=[slab] * so...  3.15 us
  transfers between devices with their start and end apart: 26, of which 12 were waited for; matrix products, arithmetic and copies ran while one was open for 0% of the time, Pallas kernels for 9%

profile of v1, /device:TPU:0, one launch (start us, length us, event | category | flops | bytes accessed | tf_op | source)
XLA Modules:
  0.0 68.5 jit_solution(7925479190606955387)
XLA Ops:
  0.7 3.1 %pack.1 = (bf16[272,128]{1,0:T(8,128)(2,1)}, bf16[272,128]{1,0:T(8,128)(2,1)}, bf16[272,128]{1,0:T(8,128)(2,1)}, bf16[272,128]{1,0:T(8,128)(2,1)}, bf16[272,128]...) custom-call(s32[2]{0:T(128)} %pad_add_fusion.place_ref, ...), custom_call_target="tpu_custom_call" | custom-call | tf_op jit(solution)/shard_map/pack/pallas_call | solution.py:276
  4.3 2.6 %collective-permute-start.1 = (bf16[272,128]{1,0:T(8,128)(2,1)}, bf16[272,128]{1,0:T(8,128)(2,1)S(1)}, u32[]{:S(2)}, u32[]{:S(2)}) collective-permute-start(bf16[272,128]{1,0:T(8,128)(2,1)} %get-tuple-element.48), channel_id=1, source_target_pairs={{0,2},{1,3},{2,0},{3,1},{4,6},{5,7},{6,4},{7,5},{8,10},{9,11},{10,... | collective-permute-start | bytes 208904 | tf_op jit(solution)/shard_map/ppermute | solution.py:297
  7.0 1.7 %collective-permute-start.3 = (bf16[272,128]{1,0:T(8,128)(2,1)}, bf16[272,128]{1,0:T(8,128)(2,1)S(1)}, u32[]{:S(2)}, u32[]{:S(2)}) collective-permute-start(bf16[272,128]{1,0:T(8,128)(2,1)} %get-tuple-element.50), channel_id=1, source_target_pairs={{0,4},{1,5},{2,6},{3,7},{4,0},{5,1},{6,2},{7,3},{8,12},{9,13},{10,... | collective-permute-start | bytes 208904 | tf_op jit(solution)/shard_map/ppermute | solution.py:297
  8.7 2.6 %collective-permute-start.5 = (bf16[272,128]{1,0:T(8,128)(2,1)}, bf16[272,128]{1,0:T(8,128)(2,1)S(1)}, u32[]{:S(2)}, u32[]{:S(2)}) collective-permute-start(bf16[272,128]{1,0:T(8,128)(2,1)} %get-tuple-element.52), channel_id=1, source_target_pairs={{0,6},{1,7},{2,4},{3,5},{4,2},{5,3},{6,0},{7,1},{8,14},{9,15},{10,... | collective-permute-start | bytes 208904 | tf_op jit(solution)/shard_map/ppermute | solution.py:297
  11.9 1.6 %collective-permute-start.7 = (bf16[272,128]{1,0:T(8,128)(2,1)}, bf16[272,128]{1,0:T(8,128)(2,1)S(1)}, u32[]{:S(2)}, u32[]{:S(2)}) collective-permute-start(bf16[272,128]{1,0:T(8,128)(2,1)} %get-tuple-element.54), channel_id=1, source_target_pairs={{0,8},{1,9},{2,10},{3,11},{4,12},{5,13},{6,14},{7,15},{8,0},{9,1},... | collective-permute-start | bytes 208904 | tf_op jit(solution)/shard_map/ppermute | solution.py:297
  13.4 1.1 %collective-permute-start.8 = (bf16[272,128]{1,0:T(8,128)(2,1)}, bf16[272,128]{1,0:T(8,128)(2,1)S(1)}, u32[]{:S(2)}, u32[]{:S(2)}) collective-permute-start(bf16[272,128]{1,0:T(8,128)(2,1)} %get-tuple-element.55), channel_id=1, source_target_pairs={{0,9},{1,8},{2,11},{3,10},{4,13},{5,12},{6,15},{7,14},{8,1},{9,0},... | collective-permute-start | bytes 208904 | tf_op jit(solution)/shard_map/ppermute | solution.py:297
  14.5 1.3 %collective-permute-start.9 = (bf16[272,128]{1,0:T(8,128)(2,1)}, bf16[272,128]{1,0:T(8,128)(2,1)S(1)}, u32[]{:S(2)}, u32[]{:S(2)}) collective-permute-start(bf16[272,128]{1,0:T(8,128)(2,1)} %get-tuple-element.56), channel_id=1, source_target_pairs={{0,10},{1,11},{2,8},{3,9},{4,14},{5,15},{6,12},{7,13},{8,2},{9,3},... | collective-permute-start | bytes 208904 | tf_op jit(solution)/shard_map/ppermute | solution.py:297
  16.1 0.7 %collective-permute-start.10 = (bf16[272,128]{1,0:T(8,128)(2,1)}, bf16[272,128]{1,0:T(8,128)(2,1)S(1)}, u32[]{:S(2)}, u32[]{:S(2)}) collective-permute-start(bf16[272,128]{1,0:T(8,128)(2,1)} %get-tuple-element.57), channel_id=1, source_target_pairs={{0,11},{1,10},{2,9},{3,8},{4,15},{5,14},{6,13},{7,12},{8,3},{9,2},... | collective-permute-start | bytes 208904 | tf_op jit(solution)/shard_map/ppermute | solution.py:297
  17.1 2.1 %collective-permute-start.11 = (bf16[272,128]{1,0:T(8,128)(2,1)}, bf16[272,128]{1,0:T(8,128)(2,1)S(1)}, u32[]{:S(2)}, u32[]{:S(2)}) collective-permute-start(bf16[272,128]{1,0:T(8,128)(2,1)} %get-tuple-element.58), channel_id=1, source_target_pairs={{0,12},{1,13},{2,14},{3,15},{4,8},{5,9},{6,10},{7,11},{8,4},{9,5},... | collective-permute-start | bytes 208904 | tf_op jit(solution)/shard_map/ppermute | solution.py:297
  19.8 2.8 %collective-permute-start.13 = (bf16[272,128]{1,0:T(8,128)(2,1)}, bf16[272,128]{1,0:T(8,128)(2,1)S(1)}, u32[]{:S(2)}, u32[]{:S(2)}) collective-permute-start(bf16[272,128]{1,0:T(8,128)(2,1)} %get-tuple-element.60), channel_id=1, source_target_pairs={{0,14},{1,15},{2,12},{3,13},{4,10},{5,11},{6,8},{7,9},{8,6},{9,7},... | collective-permute-start | bytes 208904 | tf_op jit(solution)/shard_map/ppermute | solution.py:297
  23.4 1.2 %collective-permute-done.12.refs_13_ = bf16[272,128]{1,0:T(8,128)(2,1)S(1)} collective-permute-done((bf16[272,128]{1,0:T(8,128)(2,1)}, bf16[272,128]{1,0:T(8,128)(2,1)S(1)}, u32[]{:S(2)}, u32[]{:S(2)}) %collective-permute-start.12) | collective-permute-done | bytes 69664 | tf_op jit(solution)/shard_map/ppermute | solution.py:297
  24.6 2.7 %collective-permute-done.13.refs_14_ = bf16[272,128]{1,0:T(8,128)(2,1)S(1)} collective-permute-done((bf16[272,128]{1,0:T(8,128)(2,1)}, bf16[272,128]{1,0:T(8,128)(2,1)S(1)}, u32[]{:S(2)}, u32[]{:S(2)}) %collective-permute-start.13) | collective-permute-done | bytes 69664 | tf_op jit(solution)/shard_map/ppermute | solution.py:297
  27.3 1.6 %collective-permute-done.14.refs_15_ = bf16[272,128]{1,0:T(8,128)(2,1)S(1)} collective-permute-done((bf16[272,128]{1,0:T(8,128)(2,1)}, bf16[272,128]{1,0:T(8,128)(2,1)S(1)}, u32[]{:S(2)}, u32[]{:S(2)}) %collective-permute-start.14) | collective-permute-done | bytes 69664 | tf_op jit(solution)/shard_map/ppermute | solution.py:297
  29.6 0.9 %copy-done.4 = bf16[272,128]{1,0:T(8,128)(2,1)S(1)} copy-done((bf16[272,128]{1,0:T(8,128)(2,1)S(1)}, bf16[272,128]{1,0:T(8,128)(2,1)}, u32[]{:S(2)}) %copy-start.4) | copy-done | bytes 69656
  30.5 4.4 %factors.1 = (bf16[16,272,128]{2,1,0:T(8,128)(2,1)S(1)}, bf16[2,128,128]{2,1,0:T(8,128)(2,1)S(1)}, bf16[8,2,128,128]{3,2,1,0:T(8,128)(2,1)S(1)}, f32[8,2,128,128...) custom-call(s32[2]{0:T(128)S(1)} %copy-done.1, ...), custom_call_target="tpu_custom_call" | custom-call | flops 4000000000 | bytes 4000000 | tf_op jit(solution)/shard_map/factors/pallas_call | solution.py:302
  34.9 4.5 %collective-permute-start.15 = (bf16[2,128,128]{2,1,0:T(8,128)(2,1)S(1)}, bf16[2,128,128]{2,1,0:T(8,128)(2,1)S(1)}, u32[]{:S(2)}, u32[]{:S(2)}) collective-permute-start(bf16[2,128,128]{2,1,0:T(8,128)(2,1)S(1)} %get-tuple-element.62.unused_ref), channel_id=1, source_target_pairs={{0,16},{1,17},{2,18},{3,19},{4,20},{5,21},{6,22},{7,23},{8,24},{9,... | collective-permute-start | bytes 196616 | tf_op jit(solution)/shard_map/ppermute | solution.py:320
  39.5 1.1 %gates.1 = (bf16[8,64,128]{2,1,0:T(8,128)(2,1)S(1)}, bf16[8,64,128]{2,1,0:T(8,128)(2,1)S(1)}, bf16[8,64,128]{2,1,0:T(8,128)(2,1)S(1)}, bf16[8,64,128]{2,1,0:T(8,128)(2,1)S(1)}) custom-call(s32[2]{0:T(128)S(1)} %copy-done.1, bf16[64,32,128]{2,1,0:T(8,128)(2,1)S(1)} %copy-done.3, bf16[1,128]{1,0:T(2,128)(2,1)S(1)} %bitcast.4, ...), custom_call_target="tpu_custom_call" | custom-call | flops 1000000000 | bytes 8000000 | tf_op jit(solution)/shard_map/gates/pallas_call | solution.py:336
  40.7 0.7 %collective-permute-start.20 = (bf16[8,64,128]{2,1,0:T(8,128)(2,1)S(1)}, bf16[8,64,128]{2,1,0:T(8,128)(2,1)S(1)}, u32[]{:S(2)}, u32[]{:S(2)}) collective-permute-start(bf16[8,64,128]{2,1,0:T(8,128)(2,1)S(1)} %get-tuple-element.76), channel_id=1, source_target_pairs={{0,2},{1,3},{2,0},{3,1},{4,6},{5,7},{6,4},{7,5},{8,10},{9,11},{10,... | collective-permute-start | bytes 393224 | tf_op jit(solution)/shard_map/ppermute | solution.py:348
  41.4 1.2 %collective-permute-start.21 = (bf16[8,64,128]{2,1,0:T(8,128)(2,1)S(1)}, bf16[8,64,128]{2,1,0:T(8,128)(2,1)S(1)}, u32[]{:S(2)}, u32[]{:S(2)}) collective-permute-start(bf16[8,64,128]{2,1,0:T(8,128)(2,1)S(1)} %get-tuple-element.77), channel_id=1, source_target_pairs={{0,3},{1,2},{2,1},{3,0},{4,7},{5,6},{6,5},{7,4},{8,11},{9,10},{10,... | collective-permute-start | bytes 393224 | tf_op jit(solution)/shard_map/ppermute | solution.py:348
  42.6 2.3 %spread.1 = (f32[2,8,128,128]{3,2,1,0:T(8,128)S(1)}, bf16[2,8,128,128]{3,2,1,0:T(8,128)(2,1)S(1)}, f32[2,128,128]{2,1,0:T(8,128)}) custom-call(bf16[16,272,128]{2,1,0:T(8,128)(2,1)S(1)} %get-tuple-element.63.got_ref, bf16[8,2,128,128]{3,2,1,0:T(8,128)(2,1)S(1)} %get-tuple-element.64.w_ref, f32[8,2,128,128]{3,2,1,0:T(8,128)S(1)} %get-tuple-element.65.u_ref, ...), custom_call_target="tpu_custom_call" | custom-call | flops 2000000000 | bytes 8000000 | tf_op jit(solution)/shard_map/spread/pallas_call | solution.py:322
  44.8 1.0 %join.1 = (bf16[2,2,128,128]{3,2,1,0:T(8,128)(2,1)S(1)}, bf16[2,2,128,128]{3,2,1,0:T(8,128)(2,1)S(1)}, bf16[2,2,128,128]{3,2,1,0:T(8,128)(2,1)S(1)}, bf16[2,2,128,128]{3,2,1,0:T(8,128)(2,1)S(1)}) custom-call(s32[2]{0:T(128)S(1)} %copy-done.2, bf16[2,128,128]{2,1,0:T(8,128)(2,1)S(1)} %collective-permute-done.15.state_ref, ...), custom_call_target="tpu_custom_call" | custom-call | tf_op jit(solution)/shard_map/join/pallas_call | solution.py:355
  46.4 1.3 %collective-permute-start.17 = (bf16[2,2,128,128]{3,2,1,0:T(8,128)(2,1)S(1)}, bf16[2,2,128,128]{3,2,1,0:T(8,128)(2,1)S(1)}, u32[]{:S(2)}, u32[]{:S(2)}) collective-permute-start(bf16[2,2,128,128]{3,2,1,0:T(8,128)(2,1)S(1)} %get-tuple-element.72), channel_id=1, source_target_pairs={{0,8},{4,12},{8,0},{12,4},{1,9},{5,13},{9,1},{13,5},{2,10},{6,14},... | collective-permute-start | bytes 393224 | tf_op jit(solution)/shard_map/ppermute | solution.py:365
  47.7 1.7 %collective-permute-start.18 = (bf16[2,2,128,128]{3,2,1,0:T(8,128)(2,1)S(1)}, bf16[2,2,128,128]{3,2,1,0:T(8,128)(2,1)S(1)}, u32[]{:S(2)}, u32[]{:S(2)}) collective-permute-start(bf16[2,2,128,128]{3,2,1,0:T(8,128)(2,1)S(1)} %get-tuple-element.73), channel_id=1, source_target_pairs={{0,12},{4,8},{8,4},{12,0},{1,13},{5,9},{9,5},{13,1},{2,14},{6,10},... | collective-permute-start | bytes 393224 | tf_op jit(solution)/shard_map/ppermute | solution.py:365
  49.5 2.2 %collective-permute-done.16.refs_1_ = bf16[2,2,128,128]{3,2,1,0:T(8,128)(2,1)S(1)} collective-permute-done((bf16[2,2,128,128]{3,2,1,0:T(8,128)(2,1)S(1)}, bf16[2,2,128,128]{3,2,1,0:T(8,128)(2,1)S(1)}, u32[]{:S(2)}, u32[]{:S(2)}) %collective-permute-start.16) | collective-permute-done | bytes 131104 | tf_op jit(solution)/shard_map/ppermute | solution.py:365
  51.7 1.1 %collective-permute-done.17.refs_2_ = bf16[2,2,128,128]{3,2,1,0:T(8,128)(2,1)S(1)} collective-permute-done((bf16[2,2,128,128]{3,2,1,0:T(8,128)(2,1)S(1)}, bf16[2,2,128,128]{3,2,1,0:T(8,128)(2,1)S(1)}, u32[]{:S(2)}, u32[]{:S(2)}) %collective-permute-start.17) | collective-permute-done | bytes 131104 | tf_op jit(solution)/shard_map/ppermute | solution.py:365
  52.8 2.9 %collective-permute-done.18.refs_3_ = bf16[2,2,128,128]{3,2,1,0:T(8,128)(2,1)S(1)} collective-permute-done((bf16[2,2,128,128]{3,2,1,0:T(8,128)(2,1)S(1)}, bf16[2,2,128,128]{3,2,1,0:T(8,128)(2,1)S(1)}, u32[]{:S(2)}, u32[]{:S(2)}) %collective-permute-start.18) | collective-permute-done | bytes 131104 | tf_op jit(solution)/shard_map/ppermute | solution.py:365
  55.7 1.4 %project.2 = (bf16[2,64,1024]{2,1,0:T(8,128)(2,1)S(1)}, f32[2,64,1024]{2,1,0:T(8,128)S(1)}, bf16[256,1024]{1,0:T(8,128)(2,1)S(1)}) custom-call(s32[2]{0:T(128)S(1)} %copy-done.2, bf16[2,2,128,128]{3,2,1,0:T(8,128)(2,1)S(1)} %get-tuple-element.70.refs_0_, bf16[2,2,128,128]{3,2,1,0:T(8,128)(2,1)S(1)} %collective-permute-done.16.refs_1_, ...), custom_call_target="tpu_custom_call" | custom-call | flops 1000000000 | bytes 4000000 | tf_op jit(solution)/shard_map/project/pallas_call | solution.py:376
  57.2 0.7 %project.3 = (bf16[2,64,1024]{2,1,0:T(8,128)(2,1)S(1)}, f32[2,64,1024]{2,1,0:T(8,128)S(1)}) custom-call(bf16[256,1024]{1,0:T(8,128)(2,1)S(1)} %get-tuple-element.81.rows_ref, bf16[1024,2048]{1,0:T(8,128)(2,1)S(1)} %copy-done), custom_call_target="tpu_custom_call" | custom-call | flops 1000000000 | bytes 4000000 | tf_op jit(solution)/shard_map/project/pallas_call | solution.py:385
  60.6 1.4 %collective-permute-start.25 = (bf16[1,64,1024]{2,1,0:T(8,128)(2,1)S(1)}, bf16[1,64,1024]{2,1,0:T(8,128)(2,1)S(1)}, u32[]{:S(2)}, u32[]{:S(2)}) collective-permute-start(bf16[1,64,1024]{2,1,0:T(8,128)(2,1)S(1)} %get-tuple-element.86), channel_id=1, source_target_pairs={{0,2},{1,3},{2,0},{3,1},{4,6},{5,7},{6,4},{7,5},{8,10},{9,11},{10,... | collective-permute-start | bytes 393224 | tf_op jit(solution)/shard_map/ppermute | solution.py:396
  62.0 3.6 %collective-permute-done.24.refs_2_ = bf16[1,64,1024]{2,1,0:T(8,128)(2,1)S(1)} collective-permute-done((bf16[1,64,1024]{2,1,0:T(8,128)(2,1)S(1)}, bf16[1,64,1024]{2,1,0:T(8,128)(2,1)S(1)}, u32[]{:S(2)}, u32[]{:S(2)}) %collective-permute-start.24) | collective-permute-done | bytes 131104 | tf_op jit(solution)/shard_map/ppermute | solution.py:396
  65.7 2.0 %collective-permute-done.25.refs_3_ = bf16[1,64,1024]{2,1,0:T(8,128)(2,1)S(1)} collective-permute-done((bf16[1,64,1024]{2,1,0:T(8,128)(2,1)S(1)}, bf16[1,64,1024]{2,1,0:T(8,128)(2,1)S(1)}, u32[]{:S(2)}, u32[]{:S(2)}) %collective-permute-start.25) | collective-permute-done | bytes 131104 | tf_op jit(solution)/shard_map/ppermute | solution.py:396
  67.7 0.8 %finish.1 = bf16[64,2048]{1,0:T(8,128)(2,1)} custom-call(f32[1,64,1024]{2,1,0:T(8,128)S(1)} %get-tuple-element.80.refs_0_, f32[1,64,1024]{2,1,0:T(8,128)S(1)} %get-tuple-element.84.refs_1_, bf16[1,64,1024]{2,1,0:T(8,128)(2,1)S(1)} %collective-permute-done.24.refs_2_, bf16[1,64,1024]{2,1,0:T(8,128)(2,1)S(1)} %collective-permute-done.25.refs_3_), custom_call_target="tpu_custom_call" | custom-call | tf_op jit(solution)/shard_map/finish/pallas_call | solution.py:412
  (43 shorter events, 7.8 us)
Async XLA Ops:
  3.8 4.9 %collective-permute-start = (bf16[272,128]{1,0:T(8,128)(2,1)}, bf16[272,128]{1,0:T(8,128)(2,1)S(1)}, u32[]{:S(2)}, u32[]{:S(2)}) collective-permute-start(bf16[272,128]{1,0:T(8,128)(2,1)} %get-tuple-element.47), channel_id=1, source_target_pairs={{0,1},{1,0},{2,3},{3,2},{4,5},{5,4},{6,7},{7,6},{8,9},{9,8},{10,11... | collective-permute-start | bytes 208904 | tf_op jit(solution)/shard_map/ppermute | solution.py:297
  4.3 7.0 %collective-permute-start.1 = (bf16[272,128]{1,0:T(8,128)(2,1)}, bf16[272,128]{1,0:T(8,128)(2,1)S(1)}, u32[]{:S(2)}, u32[]{:S(2)}) collective-permute-start(bf16[272,128]{1,0:T(8,128)(2,1)} %get-tuple-element.48), channel_id=1, source_target_pairs={{0,2},{1,3},{2,0},{3,1},{4,6},{5,7},{6,4},{7,5},{8,10},{9,11},{10,... | collective-permute-start | bytes 208904 | tf_op jit(solution)/shard_map/ppermute | solution.py:297
  6.9 4.9 %collective-permute-start.2 = (bf16[272,128]{1,0:T(8,128)(2,1)}, bf16[272,128]{1,0:T(8,128)(2,1)S(1)}, u32[]{:S(2)}, u32[]{:S(2)}) collective-permute-start(bf16[272,128]{1,0:T(8,128)(2,1)} %get-tuple-element.49), channel_id=1, source_target_pairs={{0,3},{1,2},{2,1},{3,0},{4,7},{5,6},{6,5},{7,4},{8,11},{9,10},{10,... | collective-permute-start | bytes 208904 | tf_op jit(solution)/shard_map/ppermute | solution.py:297
  7.0 6.5 %collective-permute-start.3 = (bf16[272,128]{1,0:T(8,128)(2,1)}, bf16[272,128]{1,0:T(8,128)(2,1)S(1)}, u32[]{:S(2)}, u32[]{:S(2)}) collective-permute-start(bf16[272,128]{1,0:T(8,128)(2,1)} %get-tuple-element.50), channel_id=1, source_target_pairs={{0,4},{1,5},{2,6},{3,7},{4,0},{5,1},{6,2},{7,3},{8,12},{9,13},{10,... | collective-permute-start | bytes 208904 | tf_op jit(solution)/shard_map/ppermute | solution.py:297
  8.7 5.8 %collective-permute-start.4 = (bf16[272,128]{1,0:T(8,128)(2,1)}, bf16[272,128]{1,0:T(8,128)(2,1)S(1)}, u32[]{:S(2)}, u32[]{:S(2)}) collective-permute-start(bf16[272,128]{1,0:T(8,128)(2,1)} %get-tuple-element.51), channel_id=1, source_target_pairs={{0,5},{1,4},{2,7},{3,6},{4,1},{5,0},{6,3},{7,2},{8,13},{9,12},{10,... | collective-permute-start | bytes 208904 | tf_op jit(solution)/shard_map/ppermute | solution.py:297
  8.7 7.4 %collective-permute-start.5 = (bf16[272,128]{1,0:T(8,128)(2,1)}, bf16[272,128]{1,0:T(8,128)(2,1)S(1)}, u32[]{:S(2)}, u32[]{:S(2)}) collective-permute-start(bf16[272,128]{1,0:T(8,128)(2,1)} %get-tuple-element.52), channel_id=1, source_target_pairs={{0,6},{1,7},{2,4},{3,5},{4,2},{5,3},{6,0},{7,1},{8,14},{9,15},{10,... | collective-permute-start | bytes 208904 | tf_op jit(solution)/shard_map/ppermute | solution.py:297
  11.4 5.7 %collective-permute-start.6 = (bf16[272,128]{1,0:T(8,128)(2,1)}, bf16[272,128]{1,0:T(8,128)(2,1)S(1)}, u32[]{:S(2)}, u32[]{:S(2)}) collective-permute-start(bf16[272,128]{1,0:T(8,128)(2,1)} %get-tuple-element.53), channel_id=1, source_target_pairs={{0,7},{1,6},{2,5},{3,4},{4,3},{5,2},{6,1},{7,0},{8,15},{9,14},{10,... | collective-permute-start | bytes 208904 | tf_op jit(solution)/shard_map/ppermute | solution.py:297
  11.9 7.3 %collective-permute-start.7 = (bf16[272,128]{1,0:T(8,128)(2,1)}, bf16[272,128]{1,0:T(8,128)(2,1)S(1)}, u32[]{:S(2)}, u32[]{:S(2)}) collective-permute-start(bf16[272,128]{1,0:T(8,128)(2,1)} %get-tuple-element.54), channel_id=1, source_target_pairs={{0,8},{1,9},{2,10},{3,11},{4,12},{5,13},{6,14},{7,15},{8,0},{9,1},... | collective-permute-start | bytes 208904 | tf_op jit(solution)/shard_map/ppermute | solution.py:297
  13.4 6.4 %collective-permute-start.8 = (bf16[272,128]{1,0:T(8,128)(2,1)}, bf16[272,128]{1,0:T(8,128)(2,1)S(1)}, u32[]{:S(2)}, u32[]{:S(2)}) collective-permute-start(bf16[272,128]{1,0:T(8,128)(2,1)} %get-tuple-element.55), channel_id=1, source_target_pairs={{0,9},{1,8},{2,11},{3,10},{4,13},{5,12},{6,15},{7,14},{8,1},{9,0},... | collective-permute-start | bytes 208904 | tf_op jit(solution)/shard_map/ppermute | solution.py:297
  14.5 8.1 %collective-permute-start.9 = (bf16[272,128]{1,0:T(8,128)(2,1)}, bf16[272,128]{1,0:T(8,128)(2,1)S(1)}, u32[]{:S(2)}, u32[]{:S(2)}) collective-permute-start(bf16[272,128]{1,0:T(8,128)(2,1)} %get-tuple-element.56), channel_id=1, source_target_pairs={{0,10},{1,11},{2,8},{3,9},{4,14},{5,15},{6,12},{7,13},{8,2},{9,3},... | collective-permute-start | bytes 208904 | tf_op jit(solution)/shard_map/ppermute | solution.py:297
  16.1 7.2 %collective-permute-start.10 = (bf16[272,128]{1,0:T(8,128)(2,1)}, bf16[272,128]{1,0:T(8,128)(2,1)S(1)}, u32[]{:S(2)}, u32[]{:S(2)}) collective-permute-start(bf16[272,128]{1,0:T(8,128)(2,1)} %get-tuple-element.57), channel_id=1, source_target_pairs={{0,11},{1,10},{2,9},{3,8},{4,15},{5,14},{6,13},{7,12},{8,3},{9,2},... | collective-permute-start | bytes 208904 | tf_op jit(solution)/shard_map/ppermute | solution.py:297
  17.1 6.3 %collective-permute-start.11 = (bf16[272,128]{1,0:T(8,128)(2,1)}, bf16[272,128]{1,0:T(8,128)(2,1)S(1)}, u32[]{:S(2)}, u32[]{:S(2)}) collective-permute-start(bf16[272,128]{1,0:T(8,128)(2,1)} %get-tuple-element.58), channel_id=1, source_target_pairs={{0,12},{1,13},{2,14},{3,15},{4,8},{5,9},{6,10},{7,11},{8,4},{9,5},... | collective-permute-start | bytes 208904 | tf_op jit(solution)/shard_map/ppermute | solution.py:297
  19.2 5.4 %collective-permute-start.12 = (bf16[272,128]{1,0:T(8,128)(2,1)}, bf16[272,128]{1,0:T(8,128)(2,1)S(1)}, u32[]{:S(2)}, u32[]{:S(2)}) collective-permute-start(bf16[272,128]{1,0:T(8,128)(2,1)} %get-tuple-element.59), channel_id=1, source_target_pairs={{0,13},{1,12},{2,15},{3,14},{4,9},{5,8},{6,11},{7,10},{8,5},{9,4},... | collective-permute-start | bytes 208904 | tf_op jit(solution)/shard_map/ppermute | solution.py:297
  19.8 7.5 %collective-permute-start.13 = (bf16[272,128]{1,0:T(8,128)(2,1)}, bf16[272,128]{1,0:T(8,128)(2,1)S(1)}, u32[]{:S(2)}, u32[]{:S(2)}) collective-permute-start(bf16[272,128]{1,0:T(8,128)(2,1)} %get-tuple-element.60), channel_id=1, source_target_pairs={{0,14},{1,15},{2,12},{3,13},{4,10},{5,11},{6,8},{7,9},{8,6},{9,7},... | collective-permute-start | bytes 208904 | tf_op jit(solution)/shard_map/ppermute | solution.py:297
  22.6 6.4 %collective-permute-start.14 = (bf16[272,128]{1,0:T(8,128)(2,1)}, bf16[272,128]{1,0:T(8,128)(2,1)S(1)}, u32[]{:S(2)}, u32[]{:S(2)}) collective-permute-start(bf16[272,128]{1,0:T(8,128)(2,1)} %get-tuple-element.61), channel_id=1, source_target_pairs={{0,15},{1,14},{2,13},{3,12},{4,11},{5,10},{6,9},{7,8},{8,7},{9,6},... | collective-permute-start | bytes 208904 | tf_op jit(solution)/shard_map/ppermute | solution.py:297
  29.0 0.7 copy-start.1
  29.6 0.9 %copy-start.4 = (bf16[272,128]{1,0:T(8,128)(2,1)S(1)}, bf16[272,128]{1,0:T(8,128)(2,1)}, u32[]{:S(2)}) copy-start(bf16[272,128]{1,0:T(8,128)(2,1)} %get-tuple-element.46.refs_0_) | copy-start | bytes 208900
  30.5 8.9 %copy-start.3 = (bf16[64,32,128]{2,1,0:T(8,128)(2,1)S(1)}, bf16[64,32,128]{2,1,0:T(8,128)(2,1)}, u32[]{:S(2)}) copy-start(bf16[64,32,128]{2,1,0:T(8,128)(2,1)} %gate_ref.1) | copy-start | bytes 1572868
  30.5 8.9 %copy-start.5 = (bf16[128]{0:T(256)(128)(2,1)S(1)}, bf16[128]{0:T(256)(128)(2,1)}, u32[]{:S(2)}) copy-start(bf16[128]{0:T(256)(128)(2,1)} %param.12) | copy-start | bytes 772
  34.9 9.9 %collective-permute-start.15 = (bf16[2,128,128]{2,1,0:T(8,128)(2,1)S(1)}, bf16[2,128,128]{2,1,0:T(8,128)(2,1)S(1)}, u32[]{:S(2)}, u32[]{:S(2)}) collective-permute-start(bf16[2,128,128]{2,1,0:T(8,128)(2,1)S(1)} %get-tuple-element.62.unused_ref), channel_id=1, source_target_pairs={{0,16},{1,17},{2,18},{3,19},{4,20},{5,21},{6,22},{7,23},{8,24},{9,... | collective-permute-start | bytes 196616 | tf_op jit(solution)/shard_map/ppermute | solution.py:320
  40.6 4.2 %copy-start.2 = (s32[2]{0:T(128)S(1)}, s32[2]{0:T(128)}, u32[]{:S(2)}) copy-start(s32[2]{0:T(128)} %pad_add_fusion.place_ref) | copy-start | bytes 28
  40.6 7.1 %collective-permute-start.19 = (bf16[8,64,128]{2,1,0:T(8,128)(2,1)S(1)}, bf16[8,64,128]{2,1,0:T(8,128)(2,1)S(1)}, u32[]{:S(2)}, u32[]{:S(2)}) collective-permute-start(bf16[8,64,128]{2,1,0:T(8,128)(2,1)S(1)} %get-tuple-element.75), channel_id=1, source_target_pairs={{0,1},{1,0},{2,3},{3,2},{4,5},{5,4},{6,7},{7,6},{8,9},{9,8},{10,11... | collective-permute-start | bytes 393224 | tf_op jit(solution)/shard_map/ppermute | solution.py:348
  40.7 8.8 %collective-permute-start.20 = (bf16[8,64,128]{2,1,0:T(8,128)(2,1)S(1)}, bf16[8,64,128]{2,1,0:T(8,128)(2,1)S(1)}, u32[]{:S(2)}, u32[]{:S(2)}) collective-permute-start(bf16[8,64,128]{2,1,0:T(8,128)(2,1)S(1)} %get-tuple-element.76), channel_id=1, source_target_pairs={{0,2},{1,3},{2,0},{3,1},{4,6},{5,7},{6,4},{7,5},{8,10},{9,11},{10,... | collective-permute-start | bytes 393224 | tf_op jit(solution)/shard_map/ppermute | solution.py:348
  41.4 8.1 %collective-permute-start.21 = (bf16[8,64,128]{2,1,0:T(8,128)(2,1)S(1)}, bf16[8,64,128]{2,1,0:T(8,128)(2,1)S(1)}, u32[]{:S(2)}, u32[]{:S(2)}) collective-permute-start(bf16[8,64,128]{2,1,0:T(8,128)(2,1)S(1)} %get-tuple-element.77), channel_id=1, source_target_pairs={{0,3},{1,2},{2,1},{3,0},{4,7},{5,6},{6,5},{7,4},{8,11},{9,10},{10,... | collective-permute-start | bytes 393224 | tf_op jit(solution)/shard_map/ppermute | solution.py:348
  42.6 13.1 %copy-start = (bf16[1024,2048]{1,0:T(8,128)(2,1)S(1)}, bf16[1024,2048]{1,0:T(8,128)(2,1)}, u32[]{:S(2)}) copy-start(bf16[1024,2048]{1,0:T(8,128)(2,1)} %weight_ref.1) | copy-start | bytes 12582916
  45.9 5.8 %collective-permute-start.16 = (bf16[2,2,128,128]{3,2,1,0:T(8,128)(2,1)S(1)}, bf16[2,2,128,128]{3,2,1,0:T(8,128)(2,1)S(1)}, u32[]{:S(2)}, u32[]{:S(2)}) collective-permute-start(bf16[2,2,128,128]{3,2,1,0:T(8,128)(2,1)S(1)} %get-tuple-element.71), channel_id=1, source_target_pairs={{0,4},{4,0},{8,12},{12,8},{1,5},{5,1},{9,13},{13,9},{2,6},{6,2},{1... | collective-permute-start | bytes 393224 | tf_op jit(solution)/shard_map/ppermute | solution.py:365
  46.4 6.4 %collective-permute-start.17 = (bf16[2,2,128,128]{3,2,1,0:T(8,128)(2,1)S(1)}, bf16[2,2,128,128]{3,2,1,0:T(8,128)(2,1)S(1)}, u32[]{:S(2)}, u32[]{:S(2)}) collective-permute-start(bf16[2,2,128,128]{3,2,1,0:T(8,128)(2,1)S(1)} %get-tuple-element.72), channel_id=1, source_target_pairs={{0,8},{4,12},{8,0},{12,4},{1,9},{5,13},{9,1},{13,5},{2,10},{6,14},... | collective-permute-start | bytes 393224 | tf_op jit(solution)/shard_map/ppermute | solution.py:365
  47.7 8.0 %collective-permute-start.18 = (bf16[2,2,128,128]{3,2,1,0:T(8,128)(2,1)S(1)}, bf16[2,2,128,128]{3,2,1,0:T(8,128)(2,1)S(1)}, u32[]{:S(2)}, u32[]{:S(2)}) collective-permute-start(bf16[2,2,128,128]{3,2,1,0:T(8,128)(2,1)S(1)} %get-tuple-element.73), channel_id=1, source_target_pairs={{0,12},{4,8},{8,4},{12,0},{1,13},{5,9},{9,5},{13,1},{2,14},{6,10},... | collective-permute-start | bytes 393224 | tf_op jit(solution)/shard_map/ppermute | solution.py:365
  57.1 1.6 %collective-permute-start.22 = (bf16[2,64,1024]{2,1,0:T(8,128)(2,1)S(1)}, bf16[2,64,1024]{2,1,0:T(8,128)(2,1)S(1)}, u32[]{:S(2)}, u32[]{:S(2)}) collective-permute-start(bf16[2,64,1024]{2,1,0:T(8,128)(2,1)S(1)} %get-tuple-element.79), channel_id=1, source_target_pairs={{0,1},{1,0},{2,3},{3,2},{4,5},{5,4},{6,7},{7,6},{8,9},{9,8},{10,11... | collective-permute-start | bytes 786440 | tf_op jit(solution)/shard_map/ppermute | solution.py:396
  57.9 2.1 %collective-permute-start.23 = (bf16[2,64,1024]{2,1,0:T(8,128)(2,1)S(1)}, bf16[2,64,1024]{2,1,0:T(8,128)(2,1)S(1)}, u32[]{:S(2)}, u32[]{:S(2)}) collective-permute-start(bf16[2,64,1024]{2,1,0:T(8,128)(2,1)S(1)} %get-tuple-element.83), channel_id=1, source_target_pairs={{0,1},{1,0},{2,3},{3,2},{4,5},{5,4},{6,7},{7,6},{8,9},{9,8},{10,11... | collective-permute-start | bytes 786440 | tf_op jit(solution)/shard_map/ppermute | solution.py:396
  59.3 6.4 %collective-permute-start.24 = (bf16[1,64,1024]{2,1,0:T(8,128)(2,1)S(1)}, bf16[1,64,1024]{2,1,0:T(8,128)(2,1)S(1)}, u32[]{:S(2)}, u32[]{:S(2)}) collective-permute-start(bf16[1,64,1024]{2,1,0:T(8,128)(2,1)S(1)} %get-tuple-element.85), channel_id=1, source_target_pairs={{0,2},{1,3},{2,0},{3,1},{4,6},{5,7},{6,4},{7,5},{8,10},{9,11},{10,... | collective-permute-start | bytes 393224 | tf_op jit(solution)/shard_map/ppermute | solution.py:396
  60.6 7.1 %collective-permute-start.25 = (bf16[1,64,1024]{2,1,0:T(8,128)(2,1)S(1)}, bf16[1,64,1024]{2,1,0:T(8,128)(2,1)S(1)}, u32[]{:S(2)}, u32[]{:S(2)}) collective-permute-start(bf16[1,64,1024]{2,1,0:T(8,128)(2,1)S(1)} %get-tuple-element.86), channel_id=1, source_target_pairs={{0,2},{1,3},{2,0},{3,1},{4,6},{5,7},{6,4},{7,5},{8,10},{9,11},{10,... | collective-permute-start | bytes 393224 | tf_op jit(solution)/shard_map/ppermute | solution.py:396
